TPU v7x, 32 devices: a whole 2x2x4 slice. The times are simulated.
32 devices in a mesh: brick: 16 (over z, x, core), vec: 2 (over y).
Axes of the slice: x: 2, y: 2, z: 4, core: 2. Of those that a mesh axis runs over, the one named last changes fastest.
Arguments:
- levels: int32 [12, 512, 16, 128], P(None, 'brick'), may hold values from 0 to 255
- start_block: int32 [16, 512, 16, 128], P('vec', 'brick'), may hold values from -8 to 8
Outputs:
- alpha_blocks: float32 [1, 16, 16], replicated
- beta_blocks: float32 [1, 16, 16], replicated
- basis: float32 [16, 512, 16, 128], P('vec', 'brick')
All inputs are finite; a program needn't handle non-finite values.
Results may differ from a plain program's by a relative error of at most 0.00026.
Values sent between devices are 32-bit elements; how exact they have to be, the bound alone decides.
A program may use at most 128 MiB of HBM per device.

v0:
```python
import math

import jax
import jax.numpy as jnp
from jax import lax
from jax.sharding import PartitionSpec as P

offsets_cube = (1, 3, 9, 27)
deepest = 27
highest = lax.Precision.HIGHEST


def padded_2(value, sides, width):
    for axis, dim in sides:
        size, length = (lax.axis_size(axis), value.shape[dim])
        up = [(i, (i + 1) % size) for i in range(size - 1)]
        down = [(j, i) for i, j in up]
        last = lax.slice_in_dim(value, length - width, length, axis=dim)
        leading = lax.slice_in_dim(value, 0, width, axis=dim)
        before = lax.ppermute(last, axis, up)
        after = lax.ppermute(leading, axis, down)
        value = jnp.concatenate([before, value, after], axis=dim)
    return value


def passed_along(value, axis, by):
    size = lax.axis_size(axis)
    pairs = [(i, i + by) for i in range(size) if 0 <= i + by < size]
    return lax.ppermute(value, axis, pairs)


def forward_take(field_in, offset, axis_dim):
    length_dim = field_in.shape[axis_dim]
    widths = [(0, 0)] * field_in.ndim
    widths[axis_dim] = (0, offset)
    return lax.slice_in_dim(jnp.pad(field_in, widths), offset, offset + length_dim, axis=axis_dim)


def backward_put(field_in, offset, axis_dim):
    length_dim = field_in.shape[axis_dim]
    widths = [(0, 0)] * field_in.ndim
    widths[axis_dim] = (offset, 0)
    return lax.slice_in_dim(jnp.pad(field_in, widths), 0, length_dim, axis=axis_dim)


def local_planes(field_in, weights, result):
    for axis_dim in (2, 3):
        for position, offset in enumerate(offsets_cube):
            channel = weights[4 * (axis_dim - 1) + position]
            result = (
                result
                + channel * forward_take(field_in, offset, axis_dim)
                + backward_put(channel * field_in, offset, axis_dim)
            )
    return result


def apply_halo(field_in, weights, lower_ext):
    row_count = field_in.shape[1]
    padded = padded_2(field_in, (("brick", 1),), deepest)
    result = jnp.zeros_like(field_in)
    for position, offset in enumerate(offsets_cube):
        result = (
            result + weights[position] * padded[:, deepest + offset : deepest + offset + row_count]
        )
        result = (
            result
            + lower_ext[position, deepest - offset : deepest - offset + row_count]
            * padded[:, deepest - offset : deepest - offset + row_count]
        )
    return local_planes(field_in, weights, result)


def inner_of(left_rows, right_rows):
    return jnp.einsum("in,jn->ij", left_rows, right_rows, precision=highest)


def body(levels, start_block):
    weights = (levels.astype(jnp.float32) + 0.5) / 256.0
    lower_weights = passed_along(weights[:4, weights.shape[1] - deepest :], "brick", 1)
    lower_ext = jnp.concatenate([lower_weights, weights[:4]], axis=1)

    def affinity_apply(field_in):
        return apply_halo(field_in, weights, lower_ext)

    unit_field = jnp.ones((1,) + levels.shape[1:], jnp.float32)
    degree = affinity_apply(unit_field)[0] + 1.0
    inv_root = lax.rsqrt(degree)

    def half_step(block_in):
        return 0.5 * (block_in + inv_root * affinity_apply(inv_root * block_in))

    own_cols = start_block.shape[0]
    grid_shape = start_block.shape
    voxel_total = lax.axis_size("brick") * grid_shape[1] * grid_shape[2] * grid_shape[3]

    def to_work(block_in):
        flat_block = block_in.reshape(own_cols, -1)
        work_rows = lax.all_gather(flat_block, "vec", axis=0, tiled=True)
        return work_rows

    def from_work(work_rows):
        own_rows = lax.dynamic_slice_in_dim(
            work_rows, lax.axis_index("vec") * own_cols, own_cols, 0
        )
        return own_rows.reshape(grid_shape)

    def total_one(partial_sum):
        summed = lax.psum(partial_sum, "brick")
        return summed

    start_work = to_work(start_block.astype(jnp.float32))
    lower_factor = jnp.linalg.cholesky(total_one(inner_of(start_work, start_work)))
    current = lax.linalg.triangular_solve(lower_factor, start_work, left_side=True, lower=True)
    basis_now = from_work(current)
    image_block = to_work(half_step(half_step(basis_now)))
    coeffs = total_one(inner_of(image_block, current))
    residual = image_block - jnp.einsum("ij,jn->in", coeffs, current, precision=highest)
    gram_matrix = total_one(inner_of(residual, residual))
    lower_factor = jnp.linalg.cholesky(gram_matrix)
    following = lax.linalg.triangular_solve(lower_factor, residual, left_side=True, lower=True)
    alpha_list = [coeffs]
    beta_list = [lower_factor]
    basis_now = from_work(following)
    basis = basis_now * math.sqrt(voxel_total)
    return (jnp.stack(alpha_list), jnp.stack(beta_list), basis)


def solution(mesh):
    return jax.shard_map(
        body,
        mesh=mesh,
        in_specs=(P(None, "brick", None, None), P("vec", "brick", None, None)),
        out_specs=(P(), P(), P("vec", "brick", None, None)),
        check_vma=False,
    )
```

profile of v0, /device:TPU:0, one launch (start us, length us, event | category | flops | bytes accessed | tf_op | source)
XLA Modules:
  0.0 394.8 jit_solution(13110975925827850992)
XLA Ops:
  7.2 1.7 convert_element_type.86
  9.0 2.5 copy.14
  11.6 2.3 add_multiply_fusion
  14.9 3.3 collective-permute-start.1
  18.9 4.3 %collective-permute-start.2 = (f32[1,27,16,128]{3,2,1,0:T(8,128)}, f32[1,27,16,128]{3,2,1,0:T(8,128)}, u32[]{:S(2)}, u32[]{:S(2)}) collective-permute-start(f32[1,27,16,128]{3,2,1,0:T(8,128)} %broadcast.144), channel_id=1, source_target_pairs={{0,2},{2,4},{4,6},{6,8},{8,10},{10,12},{12,14},{14,16},{16,18},{18... | collective-permute-start | bytes 663560 | tf_op jit(solution)/shard_map/ppermute | solution.py:20
  25.5 1.6 slice_bitcast_fusion.3
  27.5 3.2 broadcast_multiply_fusion.16
  30.7 40.4 %all-gather.3.cloned.1.call-done = f32[16,65536]{1,0:T(8,128)} async-done(((f32[8,65536]{1,0:T(8,128)}), f32[16,65536]{1,0:T(8,128)}) %all-gather.3.cloned.1.call-update) | async-done | bytes 4194320 | tf_op jit(solution)/shard_map/all_gather | solution.py:99
  71.1 9.0 %fusion.134 = f32[16,16]{0,1:T(8,128)S(1)} fusion(f32[16,65536]{1,0:T(8,128)} %all-gather.3.cloned.1.call-done), kind=kOutput, calls=%fused_computation.264 | convolution fusion | flops 201326592 | bytes 4195328 | tf_op jit(solution)/shard_map/in,jn->ij/dot_general | solution.py:75
  80.1 33.7 %psum.21 = f32[16,16]{0,1:T(8,128)S(1)} all-reduce(f32[16,16]{0,1:T(8,128)S(1)} %fusion.134), channel_id=1, replica_groups=mesh['brick'=16,'vec'=2] {'brick'}, use_global_device_ids=true, to_apply=%region_0.1 | all-reduce | flops 256 | bytes 2048 | tf_op jit(solution)/shard_map/psum | solution.py:109
  113.9 1.5 cholesky.44
  117.9 5.4 %fusion.128 = f32[16,65536]{1,0:T(8,128)S(1)} fusion(f32[16,65536]{1,0:T(8,128)} %all-gather.3.cloned.1.call-done, f32[1,16,16]{1,2,0:T(8,128)S(1)} %custom-call.6), kind=kOutput, calls=%fused_computation.241 | convolution fusion | flops 201326592 | bytes 8389632 | tf_op jit(solution)/shard_map/triangular_solve/dot.1 | solution.py:114
  123.5 1.8 copy-done.1
  125.3 1.8 broadcast_multiply_fusion.14
  127.5 1.3 collective-permute-start.3
  128.8 3.3 collective-permute-start.4
  132.2 4.7 %broadcast_multiply_fusion.12 = (f32[8,32,16,128]{3,0,2,1:T(8,128)}, f32[8,32,16,128]{3,0,2,1:T(8,128)}, f32[8,32,16,128]{3,0,2,1:T(8,128)}, f32[8,32,16,128]{3,...) fusion(f32[8,32,16,128]{3,0,2,1:T(8,128)S(1)} %get-tuple-element.18, ...), kind=kLoop, calls=%fused_computation.160 | loop fusion | flops 3145728 | bytes 16252928 | tf_op jit(solution)/shard_map/mul | solution.py:53
  138.7 13.8 %broadcast_multiply_fusion.13 = (f32[8,32,16,128]{3,0,2,1:T(8,128)}, f32[8,32,16,128]{3,0,2,1:T(8,128)S(1)}, f32[8,32,16,128]{3,0,2,1:T(8,128)}) fusion(f32[32,16,128]{2,1,0:T(8,128)} %get-tuple-element.20, f32[32,16,128]{2,1,0:T(8,128)} %get-tuple-element.11, f32[8,32,16,128]{3,0,2,1:T(8,128)S(1)} %bitcast.71, f32[8,32,16,128]{3,0,2,1:T(8,128)} %get-tuple-element.52, ...), kind=kLoop, calls=%fused_computation.161 | loop fusion | flops 25690112 | bytes 33423360 | tf_op jit(solution)/shard_map/mul | solution.py:53
  153.0 1.3 collective-permute-start.5
  154.3 28.7 %collective-permute-start.6 = (f32[8,27,16,128]{3,0,2,1:T(8,128)S(1)}, f32[8,27,16,128]{3,0,2,1:T(8,128)}, u32[]{:S(2)}, u32[]{:S(2)}) collective-permute-start(f32[8,27,16,128]{3,0,2,1:T(8,128)S(1)} %get-tuple-element.39), channel_id=1, source_target_pairs={{0,2},{2,4},{4,6},{6,8},{8,10},{10,12},{12,14},{14,16},{16,18},{18... | collective-permute-start | bytes 5308424 | tf_op jit(solution)/shard_map/ppermute | solution.py:20
  183.0 4.1 %broadcast_multiply_fusion.11 = (f32[8,32,16,128]{3,0,2,1:T(8,128)S(1)}, f32[8,32,16,128]{3,0,2,1:T(8,128)}, f32[8,32,16,128]{3,0,2,1:T(8,128)}, f32[8,32,16,128...) fusion(f32[8,32,16,128]{3,0,2,1:T(8,128)S(1)} %get-tuple-element.9, ...), kind=kLoop, calls=%fused_computation.159 | loop fusion | flops 3145728 | bytes 16252928 | tf_op jit(solution)/shard_map/mul | solution.py:53
  187.1 12.0 %add_multiply_fusion.1 = f32[8,32,16,128]{3,0,2,1:T(8,128)} fusion(f32[8,32,16,128]{3,0,2,1:T(8,128)S(1)} %copy-done.3, f32[8,32,16,128]{3,0,2,1:T(8,128)} %get-tuple-element.44, f32[8,32,16,128]{3,0,2,1:T(8,128)S(1)} %get-tuple-element.9, f32[8,32,16,128]{3,0,2,1:T(8,128)} %get-tuple-element.41, f32[8,32,16,128]{3,0,2,1:T(8,128)} %get-tuple-element.42, ...), kind=kLoop, calls=%fused_computation.146 | loop fusion | flops 25690112 | bytes 28966912 | tf_op jit(solution)/shard_map/mul | solution.py:91
  199.2 89.6 %all-gather.5.cloned.1.call-done = f32[16,65536]{1,0:T(8,128)} async-done(((f32[8,65536]{1,0:T(8,128)}), f32[16,65536]{1,0:T(8,128)}) %all-gather.5.cloned.1.call-update) | async-done | bytes 4194320 | tf_op jit(solution)/shard_map/all_gather | solution.py:99
  288.8 8.6 %fusion.135 = f32[16,16]{1,0:T(8,128)S(1)} fusion(f32[16,65536]{1,0:T(8,128)} %all-gather.5.cloned.1.call-done, f32[16,65536]{1,0:T(8,128)} %copy-done.1), kind=kOutput, calls=%fused_computation.265 | convolution fusion | flops 201326592 | bytes 8389632 | tf_op jit(solution)/shard_map/in,jn->ij/dot_general | solution.py:75
  297.4 33.9 %psum.22 = f32[16,16]{1,0:T(8,128)S(1)} all-reduce(f32[16,16]{1,0:T(8,128)S(1)} %fusion.135), channel_id=1, replica_groups=mesh['brick'=16,'vec'=2] {'brick'}, use_global_device_ids=true, to_apply=%region_3.6 | all-reduce | flops 256 | bytes 2048 | tf_op jit(solution)/shard_map/psum | solution.py:109
  331.3 7.1 %convolution_subtract_fusion = f32[16,65536]{1,0:T(8,128)S(1)} fusion(f32[16,65536]{1,0:T(8,128)} %all-gather.5.cloned.1.call-done, f32[16,16]{1,0:T(8,128)S(1)} %psum.22, f32[16,65536]{1,0:T(8,128)} %copy-done.1), kind=kOutput, calls=%fused_computation | convolution fusion | flops 202375168 | bytes 12583936 | tf_op jit(solution)/shard_map/ij,jn->in/dot_general | solution.py:118
  338.5 1.9 copy-done
  340.4 5.6 %fusion.136 = f32[16,16]{0,1:T(8,128)S(1)} fusion(f32[16,65536]{1,0:T(8,128)S(1)} %convolution_subtract_fusion), kind=kOutput, calls=%fused_computation.266 | convolution fusion | flops 201326592 | bytes 4195328 | tf_op jit(solution)/shard_map/in,jn->ij/dot_general | solution.py:75
  346.0 30.0 %psum.23 = f32[16,16]{0,1:T(8,128)S(1)} all-reduce(f32[16,16]{0,1:T(8,128)S(1)} %fusion.136), channel_id=1, replica_groups=mesh['brick'=16,'vec'=2] {'brick'}, use_global_device_ids=true, to_apply=%region_4.7 | all-reduce | flops 256 | bytes 2048 | tf_op jit(solution)/shard_map/psum | solution.py:109
  376.1 1.5 cholesky.55
  380.7 5.4 %fusion.125 = f32[16,65536]{1,0:T(8,128)S(1)} fusion(f32[16,65536]{1,0:T(8,128)} %copy-done, f32[1,16,16]{1,2,0:T(8,128)S(1)} %custom-call.7), kind=kOutput, calls=%fused_computation.237 | convolution fusion | flops 201326592 | bytes 8389632 | tf_op jit(solution)/shard_map/triangular_solve/dot.1 | solution.py:121
  386.3 1.7 copy.9
  (70 shorter events, 13.3 us)
Async XLA Ops:
  7.2 64.0 %all-gather.3.cloned.1.call-start = ((), (), s32[]{:S(2)}) async-start(), calls=%async_computation | async-start | bytes 6291456 | tf_op jit(solution)/shard_map/all_gather | solution.py:99
  11.5 277.3 %all-gather.5.cloned.1.call-start = ((), (), s32[]{:S(2)}) async-start(), calls=%async_computation.1 | async-start | bytes 6291456 | tf_op jit(solution)/shard_map/all_gather | solution.py:99
  14.9 12.2 %collective-permute-start.1 = (f32[4,27,16,128]{3,2,1,0:T(8,128)}, f32[4,27,16,128]{3,2,1,0:T(8,128)}, u32[]{:S(2)}, u32[]{:S(2)}) collective-permute-start(f32[4,27,16,128]{3,2,1,0:T(8,128)} %slice.424), channel_id=1, source_target_pairs={{0,2},{2,4},{4,6},{6,8},{8,10},{10,12},{12,14},{14,16},{16,18},{18... | collective-permute-start | bytes 2654216 | tf_op jit(solution)/shard_map/ppermute | solution.py:29
  18.9 8.2 %collective-permute-start.2 = (f32[1,27,16,128]{3,2,1,0:T(8,128)}, f32[1,27,16,128]{3,2,1,0:T(8,128)}, u32[]{:S(2)}, u32[]{:S(2)}) collective-permute-start(f32[1,27,16,128]{3,2,1,0:T(8,128)} %broadcast.144), channel_id=1, source_target_pairs={{0,2},{2,4},{4,6},{6,8},{8,10},{10,12},{12,14},{14,16},{16,18},{18... | collective-permute-start | bytes 663560 | tf_op jit(solution)/shard_map/ppermute | solution.py:20
  23.2 4.0 %collective-permute-start = (f32[1,27,16,128]{3,2,1,0:T(8,128)}, f32[1,27,16,128]{3,2,1,0:T(8,128)}, u32[]{:S(2)}, u32[]{:S(2)}) collective-permute-start(f32[1,27,16,128]{3,2,1,0:T(8,128)} %broadcast.144), channel_id=1, source_target_pairs={{2,0},{4,2},{6,4},{8,6},{10,8},{12,10},{14,12},{16,14},{18,16},{20... | collective-permute-start | bytes 663560 | tf_op jit(solution)/shard_map/ppermute | solution.py:21
  25.5 2.0 copy-start.16
  123.3 1.9 copy-start.1
  123.4 1.9 copy-start.14
  123.4 1.9 copy-start.15
  127.1 5.1 %copy-start.4 = (f32[32,16,128]{2,1,0:T(8,128)S(1)}, f32[32,16,128]{2,1,0:T(8,128)}, u32[]{:S(2)}) copy-start(f32[32,16,128]{2,1,0:T(8,128)} %get-tuple-element.22) | copy-start | bytes 786436
  127.1 5.1 %copy-start.6 = (f32[32,16,128]{2,1,0:T(8,128)S(1)}, f32[32,16,128]{2,1,0:T(8,128)}, u32[]{:S(2)}) copy-start(f32[32,16,128]{2,1,0:T(8,128)} %get-tuple-element.23) | copy-start | bytes 786436
  127.1 5.1 %copy-start.8 = (f32[32,16,128]{2,1,0:T(8,128)S(1)}, f32[32,16,128]{2,1,0:T(8,128)}, u32[]{:S(2)}) copy-start(f32[32,16,128]{2,1,0:T(8,128)} %get-tuple-element.24) | copy-start | bytes 786436
  127.1 5.1 %copy-start.10 = (f32[32,16,128]{2,1,0:T(8,128)S(1)}, f32[32,16,128]{2,1,0:T(8,128)}, u32[]{:S(2)}) copy-start(f32[32,16,128]{2,1,0:T(8,128)} %get-tuple-element.25) | copy-start | bytes 786436
  127.1 5.1 %copy-start.12 = (f32[32,16,128]{2,1,0:T(8,128)S(1)}, f32[32,16,128]{2,1,0:T(8,128)}, u32[]{:S(2)}) copy-start(f32[32,16,128]{2,1,0:T(8,128)} %get-tuple-element.26) | copy-start | bytes 786436
  127.5 9.4 %collective-permute-start.3 = (f32[8,27,16,128]{3,0,2,1:T(8,128)S(1)}, f32[8,27,16,128]{3,0,2,1:T(8,128)S(1)}, u32[]{:S(2)}, u32[]{:S(2)}) collective-permute-start(f32[8,27,16,128]{3,0,2,1:T(8,128)S(1)} %get-tuple-element.46), channel_id=1, source_target_pairs={{2,0},{4,2},{6,4},{8,6},{10,8},{12,10},{14,12},{16,14},{18,16},{20... | collective-permute-start | bytes 5308424 | tf_op jit(solution)/shard_map/ppermute | solution.py:21
  128.8 8.1 %collective-permute-start.4 = (f32[8,27,16,128]{3,0,2,1:T(8,128)S(1)}, f32[8,27,16,128]{3,0,2,1:T(8,128)S(1)}, u32[]{:S(2)}, u32[]{:S(2)}) collective-permute-start(f32[8,27,16,128]{3,0,2,1:T(8,128)S(1)} %get-tuple-element.47), channel_id=1, source_target_pairs={{0,2},{2,4},{4,6},{6,8},{8,10},{10,12},{12,14},{14,16},{16,18},{18... | collective-permute-start | bytes 5308424 | tf_op jit(solution)/shard_map/ppermute | solution.py:20
  136.9 1.2 copy-start.17
  136.9 1.7 copy-start.18
  152.5 30.5 %copy-start.5 = (f32[32,16,128]{2,1,0:T(8,128)S(1)}, f32[32,16,128]{2,1,0:T(8,128)}, u32[]{:S(2)}) copy-start(f32[32,16,128]{2,1,0:T(8,128)} %get-tuple-element.22) | copy-start | bytes 786436
  152.5 30.5 %copy-start.7 = (f32[32,16,128]{2,1,0:T(8,128)S(1)}, f32[32,16,128]{2,1,0:T(8,128)}, u32[]{:S(2)}) copy-start(f32[32,16,128]{2,1,0:T(8,128)} %get-tuple-element.23) | copy-start | bytes 786436
  152.5 30.5 %copy-start.9 = (f32[32,16,128]{2,1,0:T(8,128)S(1)}, f32[32,16,128]{2,1,0:T(8,128)}, u32[]{:S(2)}) copy-start(f32[32,16,128]{2,1,0:T(8,128)} %get-tuple-element.24) | copy-start | bytes 786436
  152.5 30.5 %copy-start.11 = (f32[32,16,128]{2,1,0:T(8,128)S(1)}, f32[32,16,128]{2,1,0:T(8,128)}, u32[]{:S(2)}) copy-start(f32[32,16,128]{2,1,0:T(8,128)} %get-tuple-element.25) | copy-start | bytes 786436
  152.5 30.5 %copy-start.13 = (f32[32,16,128]{2,1,0:T(8,128)S(1)}, f32[32,16,128]{2,1,0:T(8,128)}, u32[]{:S(2)}) copy-start(f32[32,16,128]{2,1,0:T(8,128)} %get-tuple-element.26) | copy-start | bytes 786436
  153.0 34.1 %collective-permute-start.5 = (f32[8,27,16,128]{3,0,2,1:T(8,128)S(1)}, f32[8,27,16,128]{3,0,2,1:T(8,128)}, u32[]{:S(2)}, u32[]{:S(2)}) collective-permute-start(f32[8,27,16,128]{3,0,2,1:T(8,128)S(1)} %get-tuple-element.38), channel_id=1, source_target_pairs={{2,0},{4,2},{6,4},{8,6},{10,8},{12,10},{14,12},{16,14},{18,16},{20... | collective-permute-start | bytes 5308424 | tf_op jit(solution)/shard_map/ppermute | solution.py:21
  154.3 32.8 %copy-start.2 = (f32[8,32,16,128]{3,0,2,1:T(8,128)S(1)}, f32[8,32,16,128]{3,0,2,1:T(8,128)}, u32[]{:S(2)}) copy-start(f32[8,32,16,128]{3,0,2,1:T(8,128)} %get-tuple-element.8) | copy-start | bytes 6291460
  154.3 32.8 %copy-start.3 = (f32[8,32,16,128]{3,0,2,1:T(8,128)S(1)}, f32[8,32,16,128]{3,0,2,1:T(8,128)}, u32[]{:S(2)}) copy-start(f32[8,32,16,128]{3,0,2,1:T(8,128)} %get-tuple-element.10) | copy-start | bytes 6291460
  154.3 32.8 %collective-permute-start.6 = (f32[8,27,16,128]{3,0,2,1:T(8,128)S(1)}, f32[8,27,16,128]{3,0,2,1:T(8,128)}, u32[]{:S(2)}, u32[]{:S(2)}) collective-permute-start(f32[8,27,16,128]{3,0,2,1:T(8,128)S(1)} %get-tuple-element.39), channel_id=1, source_target_pairs={{0,2},{2,4},{4,6},{6,8},{8,10},{10,12},{12,14},{14,16},{16,18},{18... | collective-permute-start | bytes 5308424 | tf_op jit(solution)/shard_map/ppermute | solution.py:20
  331.3 7.1 %copy-start.19 = (f32[16,16]{1,0:T(8,128)}, f32[16,16]{1,0:T(8,128)S(1)}, u32[]{:S(2)}) copy-start(f32[16,16]{1,0:T(8,128)S(1)} %psum.22) | copy-start | bytes 3076
  338.4 1.9 copy-start
Sparse Core Ops, SparseCore 0:
  11.6 59.4 all-gather.2
  199.3 89.4 all-gather.4
where the time goes:
time: 395 us
  waiting for transfers between devices  130 us (33%)
  blocking collectives  97.6 us (25%)
  other arithmetic  54.1 us (14%)
  starting transfers between devices  43.5 us (11%)
  matrix products  41.1 us (10%)
  between operations  14.4 us (4%)
  local copies, waits for them, and re-layouts  13.9 us (4%)
    all_gather x2, waiting for transfers between devices, to_work(): work_rows = lax.all_gather(flat_block, 'vec', axis=0, tiled=True)  130 us
    psum x3, blocking collectives, total_one(): summed = lax.psum(partial_sum, 'brick')  97.6 us
    ppermute x3, starting transfers between devices, padded_2(): before = lax.ppermute(last, axis, up)  36.3 us
    mul x4, other arithmetic, local_planes(): channel * field_in  24.4 us
    dot_general x3, matrix products, inner_of(): return jnp.einsum('in,jn->ij', left_rows, right_rows, precision=highest)  23.2 us
    mul x2, other arithmetic, half_step(): return 0.5 * (block_in + inv_root * affinity_apply(inv_root * block_in))  15.3 us
    unnamed x42, local copies, waits for them, and re-layouts  10 us
  transfers between devices with their start and end apart: 9, of which 2 were waited for; matrix products, arithmetic and copies ran while one was open for 5% of the time, Pallas kernels for 0%

commit v1 on v0

v1 whole, which is shorter than its diff:
```python
import functools
import math

import jax
import jax.numpy as jnp
from jax import lax
from jax.experimental import pallas as pl
from jax.experimental.pallas import tpu as pltpu
from jax.sharding import PartitionSpec as P

offsets_cube = (1, 3, 9, 27)
deepest = 27
highest = lax.Precision.HIGHEST
GROUPS = 2
MESH = pl.DeviceIdType.MESH


def shift_up(value, axis):
    size = lax.axis_size(axis)
    return lax.ppermute(value, axis, [(i, i + 1) for i in range(size - 1)])


def shift_down(value, axis):
    size = lax.axis_size(axis)
    return lax.ppermute(value, axis, [(i + 1, i) for i in range(size - 1)])


def forward_take(field_in, offset, axis_dim):
    length_dim = field_in.shape[axis_dim]
    widths = [(0, 0)] * field_in.ndim
    widths[axis_dim] = (0, offset)
    return lax.slice_in_dim(jnp.pad(field_in, widths), offset, offset + length_dim, axis=axis_dim)


def backward_put(field_in, offset, axis_dim):
    length_dim = field_in.shape[axis_dim]
    widths = [(0, 0)] * field_in.ndim
    widths[axis_dim] = (offset, 0)
    return lax.slice_in_dim(jnp.pad(field_in, widths), 0, length_dim, axis=axis_dim)


def local_planes(field_in, weights, result):
    for axis_dim in (2, 3):
        for position, offset in enumerate(offsets_cube):
            channel = weights[4 * (axis_dim - 1) + position]
            result = (
                result
                + channel * forward_take(field_in, offset, axis_dim)
                + backward_put(channel * field_in, offset, axis_dim)
            )
    return result


def apply_padded(field_in, before, after, weights, lower_ext):
    row_count = field_in.shape[1]
    padded = jnp.concatenate([before, field_in, after], axis=1)
    result = jnp.zeros_like(field_in)
    for position, offset in enumerate(offsets_cube):
        result = (
            result + weights[position] * padded[:, deepest + offset : deepest + offset + row_count]
        )
        result = (
            result
            + lower_ext[position][:row_count]
            * padded[:, deepest - offset : deepest - offset + row_count]
        )
    return local_planes(field_in, weights, result)


def sum_kernel(bricks, vecs, own_ref, out_ref, slots, send_sem, recv_sem):
    brick = lax.axis_index("brick")
    vec = lax.axis_index("vec")
    total = bricks * vecs
    me = brick * vecs + vec

    def peer(step):
        other = lax.rem(me + step, total)
        return (other // vecs, lax.rem(other, vecs))

    barrier = pltpu.get_barrier_semaphore()

    def greet(step, carry):
        pl.semaphore_signal(barrier, inc=1, device_id=peer(step), device_id_type=MESH)
        return carry

    lax.fori_loop(1, total, greet, 0)
    pl.semaphore_wait(barrier, total - 1)

    def copy_of(step):
        return pltpu.make_async_remote_copy(
            src_ref=own_ref,
            dst_ref=slots.at[me],
            send_sem=send_sem.at[step],
            recv_sem=recv_sem.at[step],
            device_id=peer(step),
            device_id_type=MESH,
        )

    def push(step, carry):
        copy_of(step).start()
        return carry

    lax.fori_loop(1, total, push, 0)
    slots[pl.ds(me, 1)] = own_ref[...][None]

    def settle(step, carry):
        copy_of(step).wait()
        return carry

    lax.fori_loop(1, total, settle, 0)
    for half in range(vecs):
        value = slots[half]
        for other in range(1, bricks):
            value = value + slots[other * vecs + half]
        out_ref[half] = value


def all_sum(tile):
    bricks, vecs = lax.axis_size("brick"), lax.axis_size("vec")
    total = bricks * vecs
    return pl.pallas_call(
        functools.partial(sum_kernel, bricks, vecs),
        out_shape=jax.ShapeDtypeStruct((vecs,) + tile.shape, jnp.float32),
        in_specs=[pl.BlockSpec(memory_space=pltpu.VMEM)],
        out_specs=pl.BlockSpec(memory_space=pltpu.VMEM),
        scratch_shapes=[
            pltpu.VMEM((total,) + tile.shape, jnp.float32),
            pltpu.SemaphoreType.DMA((total,)),
            pltpu.SemaphoreType.DMA((total,)),
        ],
        compiler_params=pltpu.CompilerParams(collective_id=0, has_side_effects=True),
        name="sum_blocks",
    )(tile)


def body(levels, start_block):
    own_cols, rows = start_block.shape[:2]
    grid_shape = start_block.shape
    vecs = lax.axis_size("vec")
    vec = lax.axis_index("vec")
    voxel_total = lax.axis_size("brick") * rows * grid_shape[2] * grid_shape[3]
    block = own_cols * vecs

    x = start_block.astype(jnp.float32)
    flat_x = x.reshape(own_cols, -1)
    swap = [(0, 1), (1, 0)]
    weights = (levels.astype(jnp.float32) + 0.5) / 256.0
    tails = jnp.concatenate(
        [weights[k, rows - o :] for k, o in enumerate(offsets_cube)], axis=0
    )
    tails = shift_up(tails, "brick")
    x_before = shift_up(x[:, rows - deepest :], "brick")
    x_after = shift_down(x[:, :deepest], "brick")
    x_other = lax.ppermute(flat_x, "vec", swap)
    lower_ext = []
    start = 0
    for k, o in enumerate(offsets_cube):
        lower_ext.append(jnp.concatenate([tails[start : start + o], weights[k]], axis=0))
        start += o

    def is_edge(value, side):
        keep = lax.axis_index("brick") != side
        return jnp.where(keep, value, 0.0)

    ones_halo = jnp.ones((1, deepest) + grid_shape[2:], jnp.float32)
    unit_field = jnp.ones((1,) + grid_shape[1:], jnp.float32)
    degree = apply_padded(
        unit_field,
        is_edge(ones_halo, 0),
        is_edge(ones_halo, lax.axis_size("brick") - 1),
        weights,
        lower_ext,
    )
    inv_root = lax.rsqrt(degree[0] + 1.0)
    root_before = shift_up(inv_root[rows - deepest :], "brick")
    root_after = shift_down(inv_root[:deepest], "brick")

    size = own_cols // GROUPS
    y_parts, y_sent = [], []
    t_parts = []
    for g in range(GROUPS):
        cols = slice(g * size, (g + 1) * size)
        applied = apply_padded(
            inv_root * x[cols],
            root_before * x_before[cols],
            root_after * x_after[cols],
            weights,
            lower_ext,
        )
        t = 0.5 * (x[cols] + inv_root * applied)
        u = inv_root * t
        t_parts.append(
            (t, u, shift_up(u[:, rows - deepest :], "brick"), shift_down(u[:, :deepest], "brick"))
        )
    for g in range(GROUPS):
        t, u, before, after = t_parts[g]
        y = 0.5 * (t + inv_root * apply_padded(u, before, after, weights, lower_ext))
        y = y.reshape(size, -1)
        y_parts.append(y)
        y_sent.append(lax.ppermute(y, "vec", [(0, 1)]))
    y = jnp.concatenate(y_parts, axis=0)
    y_other = jnp.concatenate(y_sent, axis=0)
    first = vec == 0
    x_low = jnp.where(first, flat_x, x_other)
    x_high = jnp.where(first, x_other, flat_x)
    y_low = jnp.where(first, y, y_other)
    y_high = jnp.where(first, 0.0, y)
    x_all = jnp.concatenate([x_low, x_high], axis=0)
    y_all = jnp.concatenate([y_low, y_high], axis=0)

    def inner(left, right):
        return jnp.einsum("in,jn->ij", left, right, precision=highest)

    tile = jnp.concatenate(
        [inner(flat_x, x_all), inner(y, x_all), inner(y, y_all)], axis=1
    )
    tile = jnp.pad(tile, ((0, 0), (0, (-tile.shape[1]) % 128)))
    sums = all_sum(tile).reshape(block, -1)
    g00 = sums[:, :block]
    g10 = sums[:, block : 2 * block]
    g11 = jnp.tril(sums[:, 2 * block : 3 * block])
    g11 = g11 + jnp.tril(g11, -1).T
    gram = jnp.concatenate(
        [jnp.concatenate([g00, g10.T], axis=1), jnp.concatenate([g10, g11], axis=1)], axis=0
    )
    factor = jnp.linalg.cholesky(gram)
    inverse = lax.linalg.triangular_solve(
        factor, jnp.eye(2 * block, dtype=jnp.float32), left_side=True, lower=True
    )
    mixed = jnp.dot(inverse[:block, :block], factor[block:], precision=highest)
    alpha, beta = mixed[:, :block], mixed[:, block:]
    coeffs = lax.dynamic_slice_in_dim(inverse, block + vec * own_cols, own_cols, 0)
    coeffs = coeffs * math.sqrt(voxel_total)
    stacked = jnp.concatenate([x_all, y_all], axis=0)
    basis = jnp.dot(coeffs, stacked, precision=highest).reshape(grid_shape)
    return alpha[None], beta[None], basis


def solution(mesh):
    return jax.shard_map(
        body,
        mesh=mesh,
        in_specs=(P(None, "brick", None, None), P("vec", "brick", None, None)),
        out_specs=(P(), P(), P("vec", "brick", None, None)),
        check_vma=False,
    )
```

time: 395 us -> 198 us (0.50)
  waiting for transfers between devices: 130 us -> 26.7 us
  blocking collectives: 97.6 us -> 0 us
  matrix products: 41.1 us -> 22.8 us
  Pallas kernels: 0 us -> 16.3 us
  between operations: 14.4 us -> 1.06 us
  other arithmetic: 54.1 us -> 64.9 us
  starting transfers between devices: 43.5 us -> 48.1 us
    all_gather x2 -> x0, waiting for transfers between devices: 130 us -> none  [to_work(): work_rows = lax.all_gather(flat_block, 'vec', axis=0, tiled=True)]
    psum x3 -> x0, blocking collectives: 97.6 us -> none  [total_one(): summed = lax.psum(partial_sum, 'brick')]
    ppermute x7 -> x12, waiting for transfers between devices: 0.02 us -> 26.7 us  [the longest x2 26.6 us: body(): y_sent.append(lax.ppermute(y, 'vec', [(0, 1)]))]
    pallas_call x0 -> x1, Pallas kernels: none -> 16.3 us  [all_sum(): pl.pallas_call(functools.partial(sum_kernel, bricks, vecs), out_shape=jax...]
    another operation x2 -> x1, matrix products: 10.8 us -> 0.22 us  [body(): lax.linalg.triangular_solve(factor, jnp.eye(2 * block, dtype=jnp.float32)...]
    mul x4 -> x6, other arithmetic: 17 us -> 25.5 us  [the longest x2 13.8 us: body(): 0.5 * (t + inv_root * apply_padded(u, before, after, weights, lower_ext))]
    dot_general x4 -> x5, matrix products: 30.3 us -> 22.6 us  [the longest x3 16.4 us: inner(): return jnp.einsum('in,jn->ij', left, right, precision=highest)]
    slice x4 -> x10, local copies, waits for them, and re-layouts: 2.89 us -> 8.3 us  [the longest x4 3.28 us: body(): tails[start:start + o]]
  transfers between devices with their start and end apart: 9 -> 12, of which waited for: 2 -> 2; matrix products, arithmetic and copies ran while one was open for 5% -> 39% of each run, Pallas kernels for 0% -> 0%
where the time goes in v1:
time: 198 us; the launch traced here: 197 us
  other arithmetic  64.9 us (33%)
  starting transfers between devices  48.1 us (24%)
  waiting for transfers between devices  26.7 us (13%)
  matrix products  22.8 us (12%)
  local copies, waits for them, and re-layouts  17.5 us (9%)
  Pallas kernels  16.3 us (8%)
    ppermute x5, starting transfers between devices, shift_up(): return lax.ppermute(value, axis, [(i, i + 1) for i in range(size - 1)])  36.4 us
    ppermute x2, waiting for transfers between devices, body(): y_sent.append(lax.ppermute(y, 'vec', [(0, 1)]))  26.6 us
    mul x5, other arithmetic, local_planes(): channel * field_in  23 us
    dot_general x3, matrix products, inner(): return jnp.einsum('in,jn->ij', left, right, precision=highest)  16.4 us
    pallas_call x1, Pallas kernels, all_sum(): pl.pallas_call(functools.partial(sum_kernel, bricks, vecs), out_shape=jax...  16.3 us
    mul x2, other arithmetic, body(): 0.5 * (t + inv_root * apply_padded(u, before, after, weights, lower_ext))  13.8 us
    unnamed x41, local copies, waits for them, and re-layouts  8.33 us
    dot_general x1, matrix products, body(): basis = jnp.dot(coeffs, stacked, precision=highest).reshape(grid_shape)  6.08 us
  transfers between devices with their start and end apart: 12, of which 2 were waited for; matrix products, arithmetic and copies ran while one was open for 39% of the time, Pallas kernels for 0%

profile of v1, /device:TPU:0, one launch (start us, length us, event | category | flops | bytes accessed | tf_op | source)
XLA Modules:
  0.0 197.4 jit_solution(11474762200630136474)
XLA Ops:
  0.6 2.5 %add_multiply_fusion = f32[12,32,16,128]{3,2,1,0:T(8,128)S(1)} fusion(s32[12,32,16,128]{3,2,1,0:T(8,128)} %param.2), kind=kLoop, calls=%fused_computation.15 | loop fusion | flops 2359296 | bytes 6291456 | tf_op jit(solution)/shard_map/div | solution.py:147
  4.0 3.1 %collective-permute-start.1 = (f32[40,16,128]{2,1,0:T(8,128)}, f32[40,16,128]{2,1,0:T(8,128)}, u32[]{:S(2)}, u32[]{:S(2)}) collective-permute-start(f32[40,16,128]{2,1,0:T(8,128)} %pad_maximum_fusion.16), channel_id=1, source_target_pairs={{0,2},{2,4},{4,6},{6,8},{8,10},{10,12},{12,14},{14,16},{16,18},{18... | collective-permute-start | bytes 983048 | tf_op jit(solution)/shard_map/ppermute | solution.py:20
  7.3 2.2 %fusion.236 = (f32[8,27,16,128]{3,2,1,0:T(8,128)}, f32[8,27,16,128]{3,2,1,0:T(8,128)}) fusion(f32[8,32,16,128]{3,2,1,0:T(8,128)S(1)} %convert_element_type.121), kind=kLoop, calls=%fused_computation.464 | loop fusion | bytes 7077888 | tf_op jit(solution)/shard_map/slice | solution.py:153
  10.8 5.6 %collective-permute-start.5 = (f32[8,27,16,128]{3,2,1,0:T(8,128)}, f32[8,27,16,128]{3,2,1,0:T(8,128)}, u32[]{:S(2)}, u32[]{:S(2)}) collective-permute-start(f32[8,27,16,128]{3,2,1,0:T(8,128)} %get-tuple-element.50), channel_id=1, source_target_pairs={{0,2},{2,4},{4,6},{6,8},{8,10},{10,12},{12,14},{14,16},{16,18},{18... | collective-permute-start | bytes 5308424 | tf_op jit(solution)/shard_map/ppermute | solution.py:20
  16.4 2.5 %copy.22 = f32[1,8,512,128]{3,1,2,0:T(8,128)} copy(f32[1,8,512,128]{3,2,1,0:T(8,128)S(1)} %bitcast.99) | data formatting | bytes 4194304
  20.5 1.8 slice_bitcast_fusion.18
  25.7 4.2 %broadcast_multiply_fusion.30 = (f32[32,16,128]{2,1,0:T(8,128)}, f32[1,32,16,128]{3,2,1,0:T(8,128)S(1)}, f32[32,16,128]{2,1,0:T(8,128)S(1)}, f32[32,16,128]{2,1,...) fusion(f32[1,32,16,128]{3,2,1,0:T(8,128)S(1)} %broadcast_in_dim.17, ...), kind=kLoop, calls=%fused_computation.415 | loop fusion | flops 2883584 | bytes 6357508 | tf_op jit(solution)/shard_map/mul | solution.py:191
  31.2 3.0 %collective-permute-start.4 = (f32[27,16,128]{2,1,0:T(8,128)S(1)}, f32[27,16,128]{2,1,0:T(8,128)S(1)}, u32[]{:S(2)}, u32[]{:S(2)}) collective-permute-start(f32[27,16,128]{2,1,0:T(8,128)S(1)} %get-tuple-element.96), channel_id=1, source_target_pairs={{0,2},{2,4},{4,6},{6,8},{8,10},{10,12},{12,14},{14,16},{16,18},{18... | collective-permute-start | bytes 663560 | tf_op jit(solution)/shard_map/ppermute | solution.py:20
  35.9 4.7 %broadcast_multiply_fusion.23 = (f32[4,32,16,128]{3,2,1,0:T(8,128)}, f32[4,32,16,128]{3,2,1,0:T(8,128)}, f32[4,32,16,128]{3,2,1,0:T(8,128)}, f32[4,32,16,128]{3,...) fusion(f32[4,32,16,128]{3,2,1,0:T(8,128)S(1)} %get-tuple-elemen, ...), kind=kLoop, calls=%fused_computation.346 | loop fusion | flops 3145728 | bytes 16252928 | tf_op jit(solution)/shard_map/mul | solution.py:49
  40.5 2.9 %slice_multiply_fusion.5 = (f32[4,27,16,128]{3,2,1,0:T(8,128)}, f32[4,27,16,128]{3,2,1,0:T(8,128)}) fusion(f32[8,27,16,128]{3,2,1,0:T(8,128)} %collective-permute-done.3, f32[27,16,128]{2,1,0:T(8,128)S(1)} %collective-permute-done.2), kind=kLoop, calls=%fused_computation.322 | loop fusion | flops 442368 | bytes 3760128 | tf_op jit(solution)/shard_map/mul | solution.py:186
  43.4 2.9 %slice_multiply_fusion.4 = (f32[4,27,16,128]{3,2,1,0:T(8,128)}, f32[4,27,16,128]{3,2,1,0:T(8,128)}) fusion(f32[8,27,16,128]{3,2,1,0:T(8,128)} %collective-permute-done.5, f32[27,16,128]{2,1,0:T(8,128)S(1)} %collective-permute-done.4), kind=kLoop, calls=%fused_computation.321 | loop fusion | flops 442368 | bytes 3760128 | tf_op jit(solution)/shard_map/mul | solution.py:185
  46.4 6.4 %broadcast_multiply_fusion.28 = (f32[4,32,16,128]{3,2,1,0:T(8,128)}, f32[4,32,16,128]{3,2,1,0:T(8,128)S(1)}, f32[4,32,16,128]{3,2,1,0:T(8,128)}) fusion(f32[32,16,128]{2,1,0:T(8,128)S(1)} %copy-done.9, f32[32,16,128]{2,1,0:T(8,128)} %get-tuple-element.16, f32[4,32,16,128]{3,2,1,0:T(8,128)} %get-tuple-element.88, ...), kind=kLoop, calls=%fused_computation.351 | loop fusion | flops 12845056 | bytes 19070976 | tf_op jit(solution)/shard_map/mul | solution.py:49
  55.5 19.3 %collective-permute-start.7 = (f32[4,27,16,128]{3,2,1,0:T(8,128)}, f32[4,27,16,128]{3,2,1,0:T(8,128)}, u32[]{:S(2)}, u32[]{:S(2)}) collective-permute-start(f32[4,27,16,128]{3,2,1,0:T(8,128)} %get-tuple-element.56), channel_id=1, source_target_pairs={{0,2},{2,4},{4,6},{6,8},{8,10},{10,12},{12,14},{14,16},{16,18},{18... | collective-permute-start | bytes 2654216 | tf_op jit(solution)/shard_map/ppermute | solution.py:20
  74.8 6.3 %broadcast_multiply_fusion.26 = (f32[4,32,16,128]{3,2,1,0:T(8,128)}, f32[4,32,16,128]{3,2,1,0:T(8,128)S(1)}, f32[4,32,16,128]{3,2,1,0:T(8,128)}) fusion(f32[32,16,128]{2,1,0:T(8,128)S(1)} %copy-done.9, f32[32,16,128]{2,1,0:T(8,128)} %get-tuple-element.16, f32[4,32,16,128]{3,2,1,0:T(8,128)} %get-tuple-element.93, ...), kind=kLoop, calls=%fused_computation.349 | loop fusion | flops 12845056 | bytes 19070976 | tf_op jit(solution)/shard_map/mul | solution.py:49
  83.7 5.3 %collective-permute-start.9 = (f32[4,27,16,128]{3,2,1,0:T(8,128)}, f32[4,27,16,128]{3,2,1,0:T(8,128)}, u32[]{:S(2)}, u32[]{:S(2)}) collective-permute-start(f32[4,27,16,128]{3,2,1,0:T(8,128)} %get-tuple-element.70), channel_id=1, source_target_pairs={{0,2},{2,4},{4,6},{6,8},{8,10},{10,12},{12,14},{14,16},{16,18},{18... | collective-permute-start | bytes 2654216 | tf_op jit(solution)/shard_map/ppermute | solution.py:20
  89.1 4.0 %broadcast_multiply_fusion.22 = (f32[4,32,16,128]{3,2,1,0:T(8,128)S(1)}, f32[4,32,16,128]{3,2,1,0:T(8,128)S(1)}, f32[4,32,16,128]{3,2,1,0:T(8,128)}, f32[4,32,16...) fusion(f32[4,32,16,128]{3,2,1,0:T(8,128)S(1)} %get-tuple-elemen, ...), kind=kLoop, calls=%fused_computation.345 | loop fusion | flops 3145728 | bytes 16252928 | tf_op jit(solution)/shard_map/mul | solution.py:49
  93.1 7.9 %add_multiply_fusion.2 = f32[4,32,16,128]{3,2,1,0:T(8,128)} fusion(f32[4,32,16,128]{3,2,1,0:T(8,128)S(1)} %copy-done.16, f32[4,32,16,128]{3,2,1,0:T(8,128)} %get-tuple-element.76, f32[4,32,16,128]{3,2,1,0:T(8,128)S(1)} %get-tuple-element.9, f32[4,32,16,128]{3,2,1,0:T(8,128)} %get-tuple-element.79, f32[4,32,16,128]{3,2,1,0:T(8,128)} %get-tuple-element.78, ...), kind=kLoop, calls=%fused_computation.313 | loop fusion | flops 12845056 | bytes 16711680 | tf_op jit(solution)/shard_map/mul | solution.py:197
  101.0 2.0 %copy.24 = f32[1,4,512,128]{3,1,2,0:T(4,128)S(1)} copy(f32[1,4,512,128]{3,2,1,0:T(8,128)} %bitcast.116) | data formatting | bytes 2097152
  103.1 5.8 %add_multiply_fusion.1 = f32[4,32,16,128]{3,2,1,0:T(8,128)} fusion(f32[4,32,16,128]{3,2,1,0:T(8,128)S(1)} %copy-done.14, f32[4,32,16,128]{3,2,1,0:T(8,128)} %get-tuple-element.81, f32[4,32,16,128]{3,2,1,0:T(8,128)S(1)} %get-tuple-element.14, f32[4,32,16,128]{3,2,1,0:T(8,128)S(1)} %get-tuple-element.72, f32[4,32,16,128]{3,2,1,0:T(8,128)} %get-tuple-element.73, ...), kind=kLoop, calls=%fused_computation.311 | loop fusion | flops 12845056 | bytes 16711680 | tf_op jit(solution)/shard_map/mul | solution.py:197
  109.0 1.9 copy.23
  110.9 3.5 %collective-permute-start.10 = (f32[4,65536]{1,0:T(4,128)S(1)}, f32[4,65536]{1,0:T(4,128)S(1)}, u32[]{:S(2)}, u32[]{:S(2)}) collective-permute-start(f32[4,65536]{1,0:T(4,128)S(1)} %bitcast.102), channel_id=1, source_target_pairs={{0,1},{2,3},{4,5},{6,7},{8,9},{10,11},{12,13},{14,15},{16,17},{18,... | collective-permute-start | bytes 3145736 | tf_op jit(solution)/shard_map/ppermute | solution.py:200
  115.9 2.8 %broadcast_select_fusion.2 = (f32[8,65536]{1,0:T(8,128)S(1)}, f32[8,65536]{1,0:T(8,128)S(1)}) fusion(f32[8,65536]{1,0:T(8,128)} %collective-permute-done, pred[]{:T(512)S(6)} %eq.4, f32[1,8,512,128]{3,2,1,0:T(8,128)S(1)} %bitcast.100), kind=kLoop, calls=%fused_computation.316 | loop fusion | flops 1048576 | bytes 8388609 | tf_op jit(solution)/shard_map/jit(_where)/select_n | solution.py:204
  118.8 5.3 %fusion.14 = f32[8,16]{1,0:T(8,128)S(1)} fusion(f32[8,65536]{1,0:T(8,128)S(1)} %get-tuple-element.25, f32[8,65536]{1,0:T(8,128)S(1)} %get-tuple-element.24, f32[1,8,512,128]{3,2,1,0:T(8,128)S(1)} %bitcast.101), kind=kOutput, calls=%fused_computation.127 | convolution fusion | flops 101711872 | bytes 6291968 | tf_op jit(solution)/shard_map/in,jn->ij/dot_general | solution.py:212
  124.1 5.4 %fusion.12 = f32[8,16]{1,0:T(8,128)S(1)} fusion(f32[8,65536]{1,0:T(8,128)S(1)} %get-tuple-element.25, f32[8,65536]{1,0:T(8,128)S(1)} %get-tuple-element.24, f32[4,65536]{1,0:T(4,128)S(1)} %bitcast.107, f32[4,65536]{1,0:T(4,128)S(1)} %bitcast.103), kind=kOutput, calls=%fused_computation.13 | convolution fusion | flops 102236160 | bytes 6291968 | tf_op jit(solution)/shard_map/in,jn->ij/dot_general | solution.py:212
  129.6 4.2 %collective-permute-done.10 = f32[4,65536]{1,0:T(4,128)S(1)} collective-permute-done((f32[4,65536]{1,0:T(4,128)S(1)}, f32[4,65536]{1,0:T(4,128)S(1)}, u32[]{:S(2)}, u32[]{:S(2)}) %collective-permute-start.10) | collective-permute-done | bytes 1048608 | tf_op jit(solution)/shard_map/ppermute | solution.py:200
  133.7 22.5 %collective-permute-done.11 = f32[4,65536]{1,0:T(4,128)S(1)} collective-permute-done((f32[4,65536]{1,0:T(4,128)S(1)}, f32[4,65536]{1,0:T(4,128)S(1)}, u32[]{:S(2)}, u32[]{:S(2)}) %collective-permute-start.11) | collective-permute-done | bytes 1048608 | tf_op jit(solution)/shard_map/ppermute | solution.py:200
  157.1 5.7 %fusion.8 = f32[8,16]{1,0:T(8,128)S(1)} fusion(f32[8,65536]{1,0:T(8,128)S(1)} %get-tuple-element.48, f32[8,65536]{1,0:T(8,128)S(1)} %get-tuple-element.47, f32[4,65536]{1,0:T(4,128)S(1)} %bitcast.109, f32[4,65536]{1,0:T(4,128)S(1)} %bitcast.105), kind=kOutput, calls=%fused_computation.9 | convolution fusion | flops 102236160 | bytes 6291968 | tf_op jit(solution)/shard_map/in,jn->ij/dot_general | solution.py:212
  163.5 16.3 %sum_blocks.1 = f32[2,8,128]{2,1,0:T(8,128)} custom-call(f32[8,128]{1,0:T(8,128)} %select_maximum_fusion.own_ref), custom_call_target="tpu_custom_call" | custom-call | tf_op jit(solution)/shard_map/sum_blocks/pallas_call | solution.py:121
  181.9 2.9 %cholesky.17 = f32[32,32]{1,0:T(8,128)S(1)} custom-call(f32[32,32]{1,0:T(8,128)S(1)} %fusion.223), custom_call_target="Cholesky" | custom-call | tf_op jit(solution)/shard_map/jit(cholesky)/cholesky | solution.py:226
  186.1 2.4 %custom-call.6 = f32[1,32,32]{1,2,0:T(8,128)S(1)} custom-call(f32[1,32,32]{2,1,0:T(8,128)S(1)} %get-tuple-element.6), custom_call_target="InvertDiagBlocksLowerTriangular" | custom-call | tf_op jit(solution)/shard_map/triangular_solve | solution.py:227
  188.8 6.1 %fusion = f32[8,65536]{1,0:T(8,128)S(1)} fusion(f32[8,65536]{1,0:T(8,128)} %copy-done.11, f32[8,65536]{1,0:T(8,128)} %copy-done.10, f32[8,65536]{1,0:T(8,128)} %copy-done.3, f32[8,65536]{1,0:T(8,128)S(1)} %copy-done.2, f32[32,32]{1,0:T(8,128)S(1)} %fusion.221, s32[]{:T(128)S(6)} %select_n.62), kind=kOutput, calls=%fused_computation | convolution fusion | flops 207618304 | bytes 10489860 | tf_op jit(solution)/shard_map/dot_general | solution.py:235
  194.9 1.7 copy.9
  (86 shorter events, 23.1 us)
Async XLA Ops:
  0.6 6.5 %copy-start.17 = (s32[8,32,16,128]{3,2,1,0:T(8,128)S(1)}, s32[8,32,16,128]{3,2,1,0:T(8,128)}, u32[]{:S(2)}) copy-start(s32[8,32,16,128]{3,2,1,0:T(8,128)} %param.3) | copy-start | bytes 6291460
  3.1 17.4 %copy-start = (f32[12,32,16,128]{3,2,1,0:T(8,128)}, f32[12,32,16,128]{3,2,1,0:T(8,128)S(1)}, u32[]{:S(2)}) copy-start(f32[12,32,16,128]{3,2,1,0:T(8,128)S(1)} %add_multiply_fusion) | copy-start | bytes 9437188
  4.0 18.3 %collective-permute-start.1 = (f32[40,16,128]{2,1,0:T(8,128)}, f32[40,16,128]{2,1,0:T(8,128)}, u32[]{:S(2)}, u32[]{:S(2)}) collective-permute-start(f32[40,16,128]{2,1,0:T(8,128)} %pad_maximum_fusion.16), channel_id=1, source_target_pairs={{0,2},{2,4},{4,6},{6,8},{8,10},{10,12},{12,14},{14,16},{16,18},{18... | collective-permute-start | bytes 983048 | tf_op jit(solution)/shard_map/ppermute | solution.py:20
  9.5 31.0 %collective-permute-start.3 = (f32[8,27,16,128]{3,2,1,0:T(8,128)}, f32[8,27,16,128]{3,2,1,0:T(8,128)}, u32[]{:S(2)}, u32[]{:S(2)}) collective-permute-start(f32[8,27,16,128]{3,2,1,0:T(8,128)} %get-tuple-element.49), channel_id=1, source_target_pairs={{2,0},{4,2},{6,4},{8,6},{10,8},{12,10},{14,12},{16,14},{18,16},{20... | collective-permute-start | bytes 5308424 | tf_op jit(solution)/shard_map/ppermute | solution.py:25
  10.8 32.6 %collective-permute-start.5 = (f32[8,27,16,128]{3,2,1,0:T(8,128)}, f32[8,27,16,128]{3,2,1,0:T(8,128)}, u32[]{:S(2)}, u32[]{:S(2)}) collective-permute-start(f32[8,27,16,128]{3,2,1,0:T(8,128)} %get-tuple-element.50), channel_id=1, source_target_pairs={{0,2},{2,4},{4,6},{6,8},{8,10},{10,12},{12,14},{14,16},{16,18},{18... | collective-permute-start | bytes 5308424 | tf_op jit(solution)/shard_map/ppermute | solution.py:20
  19.0 97.0 %collective-permute-start = (f32[8,65536]{1,0:T(8,128)}, f32[8,65536]{1,0:T(8,128)}, u32[]{:S(2)}, u32[]{:S(2)}) collective-permute-start(f32[8,65536]{1,0:T(8,128)} %bitcast.96), channel_id=1, source_target_pairs={{0,1},{1,0},{2,3},{3,2},{4,5},{5,4},{6,7},{7,6},{8,9},{9,8},{10,11... | collective-permute-start | bytes 6291464 | tf_op jit(solution)/shard_map/ppermute | solution.py:154
  25.7 8.6 %copy-start.9 = (f32[32,16,128]{2,1,0:T(8,128)S(1)}, f32[32,16,128]{2,1,0:T(8,128)}, u32[]{:S(2)}) copy-start(f32[32,16,128]{2,1,0:T(8,128)} %get-tuple-element.27) | copy-start | bytes 786436
  29.9 10.6 %collective-permute-start.2 = (f32[27,16,128]{2,1,0:T(8,128)S(1)}, f32[27,16,128]{2,1,0:T(8,128)S(1)}, u32[]{:S(2)}, u32[]{:S(2)}) collective-permute-start(f32[27,16,128]{2,1,0:T(8,128)S(1)} %get-tuple-element.95), channel_id=1, source_target_pairs={{2,0},{4,2},{6,4},{8,6},{10,8},{12,10},{14,12},{16,14},{18,16},{20... | collective-permute-start | bytes 663560 | tf_op jit(solution)/shard_map/ppermute | solution.py:25
  31.2 12.2 %collective-permute-start.4 = (f32[27,16,128]{2,1,0:T(8,128)S(1)}, f32[27,16,128]{2,1,0:T(8,128)S(1)}, u32[]{:S(2)}, u32[]{:S(2)}) collective-permute-start(f32[27,16,128]{2,1,0:T(8,128)S(1)} %get-tuple-element.96), channel_id=1, source_target_pairs={{0,2},{2,4},{4,6},{6,8},{8,10},{10,12},{12,14},{14,16},{16,18},{18... | collective-permute-start | bytes 663560 | tf_op jit(solution)/shard_map/ppermute | solution.py:20
  34.3 1.6 copy-start.4
  43.4 3.0 %copy-start.5 = (f32[32,16,128]{2,1,0:T(8,128)S(1)}, f32[32,16,128]{2,1,0:T(8,128)}, u32[]{:S(2)}) copy-start(f32[32,16,128]{2,1,0:T(8,128)} %get-tuple-element.33) | copy-start | bytes 786436
  43.4 3.0 %copy-start.6 = (f32[32,16,128]{2,1,0:T(8,128)S(1)}, f32[32,16,128]{2,1,0:T(8,128)}, u32[]{:S(2)}) copy-start(f32[32,16,128]{2,1,0:T(8,128)} %get-tuple-element.42) | copy-start | bytes 786436
  43.4 3.0 %copy-start.7 = (f32[32,16,128]{2,1,0:T(8,128)S(1)}, f32[32,16,128]{2,1,0:T(8,128)}, u32[]{:S(2)}) copy-start(f32[32,16,128]{2,1,0:T(8,128)} %get-tuple-element.43) | copy-start | bytes 786436
  43.4 3.0 %copy-start.8 = (f32[32,16,128]{2,1,0:T(8,128)S(1)}, f32[32,16,128]{2,1,0:T(8,128)}, u32[]{:S(2)}) copy-start(f32[32,16,128]{2,1,0:T(8,128)} %get-tuple-element.44) | copy-start | bytes 786436
  43.4 3.0 %copy-start.12 = (f32[32,16,128]{2,1,0:T(8,128)S(1)}, f32[32,16,128]{2,1,0:T(8,128)}, u32[]{:S(2)}) copy-start(f32[32,16,128]{2,1,0:T(8,128)} %get-tuple-element.38) | copy-start | bytes 786436
  54.2 38.9 %collective-permute-start.6 = (f32[4,27,16,128]{3,2,1,0:T(8,128)}, f32[4,27,16,128]{3,2,1,0:T(8,128)}, u32[]{:S(2)}, u32[]{:S(2)}) collective-permute-start(f32[4,27,16,128]{3,2,1,0:T(8,128)} %get-tuple-element.55), channel_id=1, source_target_pairs={{2,0},{4,2},{6,4},{8,6},{10,8},{12,10},{14,12},{16,14},{18,16},{20... | collective-permute-start | bytes 2654216 | tf_op jit(solution)/shard_map/ppermute | solution.py:25
  55.5 37.6 %collective-permute-start.7 = (f32[4,27,16,128]{3,2,1,0:T(8,128)}, f32[4,27,16,128]{3,2,1,0:T(8,128)}, u32[]{:S(2)}, u32[]{:S(2)}) collective-permute-start(f32[4,27,16,128]{3,2,1,0:T(8,128)} %get-tuple-element.56), channel_id=1, source_target_pairs={{0,2},{2,4},{4,6},{6,8},{8,10},{10,12},{12,14},{14,16},{16,18},{18... | collective-permute-start | bytes 2654216 | tf_op jit(solution)/shard_map/ppermute | solution.py:20
  82.4 20.6 %collective-permute-start.8 = (f32[4,27,16,128]{3,2,1,0:T(8,128)}, f32[4,27,16,128]{3,2,1,0:T(8,128)}, u32[]{:S(2)}, u32[]{:S(2)}) collective-permute-start(f32[4,27,16,128]{3,2,1,0:T(8,128)} %get-tuple-element.69), channel_id=1, source_target_pairs={{2,0},{4,2},{6,4},{8,6},{10,8},{12,10},{14,12},{16,14},{18,16},{20... | collective-permute-start | bytes 2654216 | tf_op jit(solution)/shard_map/ppermute | solution.py:25
  83.7 9.3 %copy-start.15 = (f32[4,32,16,128]{3,2,1,0:T(8,128)S(1)}, f32[4,32,16,128]{3,2,1,0:T(8,128)}, u32[]{:S(2)}) copy-start(f32[4,32,16,128]{3,2,1,0:T(8,128)} %get-tuple-element.8) | copy-start | bytes 3145732
  83.7 9.3 %copy-start.16 = (f32[4,32,16,128]{3,2,1,0:T(8,128)S(1)}, f32[4,32,16,128]{3,2,1,0:T(8,128)}, u32[]{:S(2)}) copy-start(f32[4,32,16,128]{3,2,1,0:T(8,128)} %get-tuple-element.10) | copy-start | bytes 3145732
  83.7 19.3 %collective-permute-start.9 = (f32[4,27,16,128]{3,2,1,0:T(8,128)}, f32[4,27,16,128]{3,2,1,0:T(8,128)}, u32[]{:S(2)}, u32[]{:S(2)}) collective-permute-start(f32[4,27,16,128]{3,2,1,0:T(8,128)} %get-tuple-element.70), channel_id=1, source_target_pairs={{0,2},{2,4},{4,6},{6,8},{8,10},{10,12},{12,14},{14,16},{16,18},{18... | collective-permute-start | bytes 2654216 | tf_op jit(solution)/shard_map/ppermute | solution.py:20
  101.0 2.1 %copy-start.13 = (f32[4,32,16,128]{3,2,1,0:T(8,128)S(1)}, f32[4,32,16,128]{3,2,1,0:T(8,128)}, u32[]{:S(2)}) copy-start(f32[4,32,16,128]{3,2,1,0:T(8,128)} %get-tuple-element.13) | copy-start | bytes 3145732
  101.0 2.1 %copy-start.14 = (f32[4,32,16,128]{3,2,1,0:T(8,128)S(1)}, f32[4,32,16,128]{3,2,1,0:T(8,128)}, u32[]{:S(2)}) copy-start(f32[4,32,16,128]{3,2,1,0:T(8,128)} %get-tuple-element.15) | copy-start | bytes 3145732
  110.9 22.9 %collective-permute-start.10 = (f32[4,65536]{1,0:T(4,128)S(1)}, f32[4,65536]{1,0:T(4,128)S(1)}, u32[]{:S(2)}, u32[]{:S(2)}) collective-permute-start(f32[4,65536]{1,0:T(4,128)S(1)} %bitcast.102), channel_id=1, source_target_pairs={{0,1},{2,3},{4,5},{6,7},{8,9},{10,11},{12,13},{14,15},{16,17},{18,... | collective-permute-start | bytes 3145736 | tf_op jit(solution)/shard_map/ppermute | solution.py:200
  114.4 41.9 %collective-permute-start.11 = (f32[4,65536]{1,0:T(4,128)S(1)}, f32[4,65536]{1,0:T(4,128)S(1)}, u32[]{:S(2)}, u32[]{:S(2)}) collective-permute-start(f32[4,65536]{1,0:T(4,128)S(1)} %bitcast.106), channel_id=1, source_target_pairs={{0,1},{2,3},{4,5},{6,7},{8,9},{10,11},{12,13},{14,15},{16,17},{18,... | collective-permute-start | bytes 3145736 | tf_op jit(solution)/shard_map/ppermute | solution.py:200
  118.8 5.3 %copy-start.1 = (f32[8,65536]{1,0:T(8,128)}, f32[8,65536]{1,0:T(8,128)S(1)}, u32[]{:S(2)}) copy-start(f32[8,65536]{1,0:T(8,128)S(1)} %get-tuple-element.24) | copy-start | bytes 6291460
  118.8 5.3 %copy-start.3 = (f32[8,65536]{1,0:T(8,128)}, f32[8,65536]{1,0:T(8,128)S(1)}, u32[]{:S(2)}) copy-start(f32[8,65536]{1,0:T(8,128)S(1)} %get-tuple-element.25) | copy-start | bytes 6291460
  157.1 5.7 %copy-start.10 = (f32[8,65536]{1,0:T(8,128)}, f32[8,65536]{1,0:T(8,128)S(1)}, u32[]{:S(2)}) copy-start(f32[8,65536]{1,0:T(8,128)S(1)} %get-tuple-element.47) | copy-start | bytes 6291460
  157.1 5.7 %copy-start.11 = (f32[8,65536]{1,0:T(8,128)}, f32[8,65536]{1,0:T(8,128)S(1)}, u32[]{:S(2)}) copy-start(f32[8,65536]{1,0:T(8,128)S(1)} %get-tuple-element.48) | copy-start | bytes 6291460
  157.1 31.7 %copy-start.2 = (f32[8,65536]{1,0:T(8,128)S(1)}, f32[8,65536]{1,0:T(8,128)}, u32[]{:S(2)}) copy-start(f32[8,65536]{1,0:T(8,128)} %copy-done.1) | copy-start | bytes 6291460

commit v2 on v1

v2 whole, which is shorter than its diff:
```python
import functools
import math

import jax
import jax.numpy as jnp
from jax import lax
from jax.experimental import pallas as pl
from jax.experimental.pallas import tpu as pltpu
from jax.sharding import PartitionSpec as P

offsets_cube = (1, 3, 9, 27)
deepest = 27
highest = lax.Precision.HIGHEST
MESH = pl.DeviceIdType.MESH


def sum_kernel(bricks, vecs, own_ref, out_ref, slots, send_sem, recv_sem):
    brick = lax.axis_index("brick")
    vec = lax.axis_index("vec")
    total = bricks * vecs
    me = brick * vecs + vec

    def peer(step):
        other = lax.rem(me + step, total)
        return (other // vecs, lax.rem(other, vecs))

    barrier = pltpu.get_barrier_semaphore()

    def greet(step, carry):
        pl.semaphore_signal(barrier, inc=1, device_id=peer(step), device_id_type=MESH)
        return carry

    lax.fori_loop(1, total, greet, 0)
    pl.semaphore_wait(barrier, total - 1)

    def copy_of(step):
        return pltpu.make_async_remote_copy(
            src_ref=own_ref,
            dst_ref=slots.at[me],
            send_sem=send_sem.at[step],
            recv_sem=recv_sem.at[step],
            device_id=peer(step),
            device_id_type=MESH,
        )

    def push(step, carry):
        copy_of(step).start()
        return carry

    lax.fori_loop(1, total, push, 0)
    slots[pl.ds(me, 1)] = own_ref[...][None]

    def settle(step, carry):
        copy_of(step).wait()
        return carry

    lax.fori_loop(1, total, settle, 0)
    for half in range(vecs):
        value = slots[half]
        for other in range(1, bricks):
            value = value + slots[other * vecs + half]
        out_ref[half] = value


def all_sum(tile):
    bricks, vecs = lax.axis_size("brick"), lax.axis_size("vec")
    total = bricks * vecs
    return pl.pallas_call(
        functools.partial(sum_kernel, bricks, vecs),
        out_shape=jax.ShapeDtypeStruct((vecs,) + tile.shape, jnp.float32),
        in_specs=[pl.BlockSpec(memory_space=pltpu.VMEM)],
        out_specs=pl.BlockSpec(memory_space=pltpu.VMEM),
        scratch_shapes=[
            pltpu.VMEM((total,) + tile.shape, jnp.float32),
            pltpu.SemaphoreType.DMA((total,)),
            pltpu.SemaphoreType.DMA((total,)),
        ],
        compiler_params=pltpu.CompilerParams(collective_id=0, has_side_effects=True),
        name="sum_blocks",
    )(tile)


ROW_STEP = 4


def fused_kernel(
    bricks, lev_ref, start_ref, x_ref, xo_ref, y_ref, yo_ref, tile_ref,
    x_low, x_high, u_one, u_two, x_weights, fore, back, root, send_sem, recv_sem,
):
    cols, rows, ny, nz = start_ref.shape
    far = deepest
    step = ROW_STEP
    brick = lax.axis_index("brick")
    vec = lax.axis_index("vec")
    has_low = brick > 0
    has_high = brick < bricks - 1
    low, high = {"brick": brick - 1}, {"brick": brick + 1}
    partner = {"vec": 1 - vec}

    def remote(src, dst, kind, slot, device):
        return pltpu.make_async_remote_copy(
            src_ref=src,
            dst_ref=dst,
            send_sem=send_sem.at[kind, slot],
            recv_sem=recv_sem.at[kind, slot],
            device_id=device,
            device_id_type=MESH,
        )

    def x_up(c):
        return remote(x_ref.at[c, pl.ds(rows - far, far)], x_low.at[c], 0, c, high)

    def x_down(c):
        return remote(x_ref.at[c, pl.ds(0, far)], x_high.at[c], 1, c, low)

    def x_over(c):
        return remote(x_ref.at[c], xo_ref.at[c], 2, c, partner)

    def u_up(c):
        return remote(u_two.at[c, pl.ds(rows, far)], u_two.at[c, pl.ds(0, far)], 3, c, high)

    def u_down(c):
        return remote(
            u_two.at[c, pl.ds(far, far)], u_two.at[c, pl.ds(far + rows, far)], 4, c, low
        )

    def y_over(c):
        return remote(y_ref.at[c], yo_ref.at[c], 5, c, partner)

    def tail_up(k):
        o = offsets_cube[k]
        return remote(
            x_weights.at[k, pl.ds(far + rows - o, o)],
            x_weights.at[k, pl.ds(far - o, o)],
            6,
            k,
            high,
        )

    def root_up():
        return remote(root.at[pl.ds(rows, far)], root.at[pl.ds(0, far)], 6, 4, high)

    def root_down():
        return remote(root.at[pl.ds(far, far)], root.at[pl.ds(far + rows, far)], 6, 5, low)

    barrier = pltpu.get_barrier_semaphore()

    def greet(device):
        pl.semaphore_signal(barrier, inc=1, device_id=device, device_id_type=MESH)

    greet(partner)
    pl.when(has_low)(lambda: greet(low))
    pl.when(has_high)(lambda: greet(high))

    def weights_of(channel, place):
        return (lev_ref[channel, place].astype(jnp.float32) + 0.5) * (1.0 / 256.0)

    def prepare_x(r, carry):
        place = pl.ds(r * step, step)
        for k in range(4):
            x_weights[k, pl.ds(far + r * step, step)] = weights_of(k, place)
        return carry

    lax.fori_loop(0, rows // step, prepare_x, 0)

    def cast(c, carry):
        x_ref[c] = start_ref[c].astype(jnp.float32)
        return carry

    lax.fori_loop(0, cols, cast, 0)
    pl.semaphore_wait(
        barrier, 1 + jnp.where(has_low, 1, 0) + jnp.where(has_high, 1, 0)
    )

    @pl.when(has_high)
    def _():
        for k in range(4):
            tail_up(k).start()

    def push_x(c, carry):
        pl.when(has_high)(lambda: x_up(c).start())
        pl.when(has_low)(lambda: x_down(c).start())
        x_over(c).start()
        return carry

    lax.fori_loop(0, cols, push_x, 0)

    edge = jnp.zeros((far, ny, nz), jnp.float32)

    @pl.when(jnp.logical_not(has_low))
    def _():
        root[pl.ds(0, far)] = edge
        for k in range(4):
            x_weights[k, pl.ds(0, far)] = edge
        for c in range(cols):
            x_low[c] = edge
            u_two[c, pl.ds(0, far)] = edge

    @pl.when(jnp.logical_not(has_high))
    def _():
        root[pl.ds(far + rows, far)] = edge
        for c in range(cols):
            x_high[c] = edge
            u_two[c, pl.ds(far + rows, far)] = edge

    lane = (step, ny, nz)
    along = [lax.broadcasted_iota(jnp.int32, lane, axis) for axis in range(3)]

    def prepare_rest(r, carry):
        place = pl.ds(r * step, step)
        degree = jnp.ones(lane, jnp.float32)
        for axis, length in ((1, ny), (2, nz)):
            for k, o in enumerate(offsets_cube):
                if o >= length:
                    continue
                channel = 4 * (axis - 1) + k
                weight = weights_of(channel + 4, place)
                forward = jnp.where(along[axis] < length - o, weight, 0.0)
                backward = pltpu.roll(forward, o, axis)
                fore[channel, place] = forward
                back[channel, place] = backward
                degree = degree + forward + backward
        root[pl.ds(far + r * step, step)] = degree
        return carry

    lax.fori_loop(0, rows // step, prepare_rest, 0)

    @pl.when(has_low)
    def _():
        for k in range(4):
            tail_up(k).wait_recv()

    limit = jnp.where(has_high, rows + far + 1, rows)

    def prepare_root(r, carry):
        place = pl.ds(far + r * step, step)
        degree = root[place]
        for k, o in enumerate(offsets_cube):
            inside = along[0] + (r * step + o) < limit
            degree = degree + jnp.where(inside, x_weights[k, place], 0.0)
            degree = degree + x_weights[k, pl.ds(far + r * step - o, step)]
        root[place] = lax.rsqrt(degree)
        return carry

    lax.fori_loop(0, rows // step, prepare_root, 0)
    pl.when(has_high)(lambda: root_up().start())
    pl.when(has_low)(lambda: root_down().start())

    def stencil(u_ref, r):
        at = far + r * step
        center = u_ref[pl.ds(at, step)]
        total = jnp.zeros(lane, jnp.float32)
        for k, o in enumerate(offsets_cube):
            total = total + x_weights[k, pl.ds(at, step)] * u_ref[pl.ds(at + o, step)]
            total = total + x_weights[k, pl.ds(at - o, step)] * u_ref[pl.ds(at - o, step)]
        place = pl.ds(r * step, step)
        for axis, length in ((1, ny), (2, nz)):
            for k, o in enumerate(offsets_cube):
                if o >= length:
                    continue
                channel = 4 * (axis - 1) + k
                total = total + fore[channel, place] * pltpu.roll(center, length - o, axis)
                total = total + back[channel, place] * pltpu.roll(center, o, axis)
        return root[pl.ds(at, step)] * total

    pl.when(has_low)(lambda: root_up().wait_recv())
    pl.when(has_high)(lambda: root_down().wait_recv())

    def first_half(c, carry):
        u_one[pl.ds(far, rows)] = root[pl.ds(far, rows)] * x_ref[c]
        pl.when(has_low)(lambda: x_up(c).wait_recv())
        u_one[pl.ds(0, far)] = root[pl.ds(0, far)] * x_low[c]
        pl.when(has_high)(lambda: x_down(c).wait_recv())
        u_one[pl.ds(far + rows, far)] = root[pl.ds(far + rows, far)] * x_high[c]

        def one(r, inner):
            place = pl.ds(r * step, step)
            image = 0.5 * (x_ref[c, place] + stencil(u_one, r))
            y_ref[c, place] = image
            at = pl.ds(far + r * step, step)
            u_two[c, at] = root[at] * image
            return inner

        lax.fori_loop(0, rows // step, one, 0)
        pl.when(has_high)(lambda: u_up(c).start())
        pl.when(has_low)(lambda: u_down(c).start())
        return carry

    lax.fori_loop(0, cols, first_half, 0)

    column = lax.broadcasted_iota(jnp.int32, tile_ref.shape, 1)

    def products(left_ref, right_ref, base, tile, ready=None):
        def one(j, tile):
            if ready is not None:
                ready(j)

            def add(r, total):
                return total + left_ref[:, r] * right_ref[j, r][None]

            total = lax.fori_loop(
                0, rows, add, jnp.zeros((cols, ny, nz), jnp.float32), unroll=2
            )
            value = jnp.sum(jnp.sum(total, axis=1), axis=1, keepdims=True)
            return jnp.where(column == base + j, value, tile)

        return lax.fori_loop(0, cols, one, tile)

    tile = products(x_ref, x_ref, 0, jnp.zeros(tile_ref.shape, jnp.float32))

    def second_half(c, carry):
        pl.when(has_low)(lambda: u_up(c).wait_recv())
        pl.when(has_high)(lambda: u_down(c).wait_recv())

        def one(r, inner):
            place = pl.ds(r * step, step)
            y_ref[c, place] = 0.5 * (y_ref[c, place] + stencil(u_two.at[c], r))
            return inner

        lax.fori_loop(0, rows // step, one, 0)
        pl.when(vec == 0)(lambda: y_over(c).start())
        return carry

    lax.fori_loop(0, cols, second_half, 0)
    tile = products(x_ref, xo_ref, cols, tile, lambda j: x_over(j).wait_recv())
    tile = products(y_ref, x_ref, 2 * cols, tile)
    tile = products(y_ref, xo_ref, 3 * cols, tile)
    tile = products(y_ref, y_ref, 4 * cols, tile)
    tile_ref[...] = tile

    @pl.when(vec == 1)
    def _():
        tile_ref[...] = products(
            y_ref, yo_ref, 5 * cols, tile_ref[...], lambda j: y_over(j).wait_recv()
        )

    @pl.when(vec == 0)
    def _():
        for c in range(cols):
            yo_ref[c] = jnp.zeros((rows, ny, nz), jnp.float32)

    def finish(c, carry):
        x_over(c).wait_send()

        @pl.when(has_high)
        def _():
            x_up(c).wait_send()
            u_up(c).wait_send()

        @pl.when(has_low)
        def _():
            x_down(c).wait_send()
            u_down(c).wait_send()

        pl.when(vec == 0)(lambda: y_over(c).wait_send())
        return carry

    lax.fori_loop(0, cols, finish, 0)

    @pl.when(has_high)
    def _():
        for k in range(4):
            tail_up(k).wait_send()
        root_up().wait_send()

    pl.when(has_low)(lambda: root_down().wait_send())


def fused(levels, start_block):
    cols, rows, ny, nz = start_block.shape
    far = deepest
    field = jax.ShapeDtypeStruct(start_block.shape, jnp.float32)
    in_vmem = pl.BlockSpec(memory_space=pltpu.VMEM)
    plane = (ny, nz)

    def room(*lead):
        return pltpu.VMEM(lead + plane, jnp.float32)

    return pl.pallas_call(
        functools.partial(fused_kernel, lax.axis_size("brick")),
        out_shape=(field,) * 4 + (jax.ShapeDtypeStruct((cols, 128), jnp.float32),),
        in_specs=[in_vmem] * 2,
        out_specs=(in_vmem,) * 5,
        scratch_shapes=[
            room(cols, far),
            room(cols, far),
            room(rows + 2 * far),
            room(cols, rows + 2 * far),
            room(4, rows + far),
            room(8, rows),
            room(8, rows),
            room(rows + 2 * far),
            pltpu.SemaphoreType.DMA((7, max(cols, 6))),
            pltpu.SemaphoreType.DMA((7, max(cols, 6))),
        ],
        compiler_params=pltpu.CompilerParams(
            collective_id=1, has_side_effects=True, vmem_limit_bytes=56 * 2**20
        ),
        name="filter_block",
    )(levels, start_block)


def body(levels, start_block):
    own_cols, rows = start_block.shape[:2]
    grid_shape = start_block.shape
    vecs = lax.axis_size("vec")
    vec = lax.axis_index("vec")
    voxel_total = lax.axis_size("brick") * rows * grid_shape[2] * grid_shape[3]
    block = own_cols * vecs
    x, x_other, y, y_other, tile = fused(levels, start_block)
    first = vec == 0
    sums = all_sum(tile)
    pairs = sums[:, :, : 6 * own_cols].reshape(vecs, own_cols, 3, 2, own_cols)
    turned = jnp.stack([pairs[0], pairs[1, :, :, ::-1]])
    sums = turned.reshape(block, 3, block)
    g00 = sums[:, 0]
    g10 = sums[:, 1]
    g11 = jnp.tril(sums[:, 2])
    g11 = g11 + jnp.tril(g11, -1).T
    gram = jnp.concatenate(
        [jnp.concatenate([g00, g10.T], axis=1), jnp.concatenate([g10, g11], axis=1)], axis=0
    )
    factor = jnp.linalg.cholesky(gram)
    inverse = lax.linalg.triangular_solve(
        factor, jnp.eye(2 * block, dtype=jnp.float32), left_side=True, lower=True
    )
    mixed = jnp.dot(inverse[:block, :block], factor[block:], precision=highest)
    alpha, beta = mixed[:, :block], mixed[:, block:]
    coeffs = lax.dynamic_slice_in_dim(inverse, block + vec * own_cols, own_cols, 0)
    coeffs = coeffs * math.sqrt(voxel_total)
    basis = combine(coeffs, vec, x, x_other, y, y_other)
    return alpha[None], beta[None], basis


def combine_kernel(coeff_ref, x_ref, xo_ref, y_ref, yo_ref, out_ref):
    cols, rows = out_ref.shape[:2]

    def one(r, carry):
        total = [jnp.zeros(out_ref.shape[2:], jnp.float32) for _ in range(cols)]
        for part, ref in enumerate((x_ref, xo_ref, y_ref, yo_ref)):
            for j in range(cols):
                value = ref[j, r]
                for i in range(cols):
                    total[i] = total[i] + coeff_ref[i, part * cols + j] * value
        for i in range(cols):
            out_ref[i, r] = total[i]
        return carry

    lax.fori_loop(0, rows, one, 0)


def combine(coeffs, vec, x, x_other, y, y_other):
    cols, rows, ny, nz = x.shape
    parts = coeffs.reshape(cols, 2, 2, cols)
    parts = jnp.where(vec == 0, parts, parts[:, :, ::-1]).reshape(cols, 4 * cols)
    slab = math.gcd(rows, 8)
    spec = pl.BlockSpec((cols, slab, ny, nz), lambda i: (0, i, 0, 0))
    return pl.pallas_call(
        combine_kernel,
        grid=(rows // slab,),
        out_shape=jax.ShapeDtypeStruct(x.shape, jnp.float32),
        in_specs=[pl.BlockSpec(memory_space=pltpu.SMEM)] + [spec] * 4,
        out_specs=spec,
        name="combine",
    )(parts, x, x_other, y, y_other)


def solution(mesh):
    return jax.shard_map(
        body,
        mesh=mesh,
        in_specs=(P(None, "brick", None, None), P("vec", "brick", None, None)),
        out_specs=(P(), P(), P("vec", "brick", None, None)),
        check_vma=False,
    )
```

time: 198 us -> 158 us (0.80)
  Pallas kernels: 16.3 us -> 147 us
  other arithmetic: 64.9 us -> 6.98 us
  starting transfers between devices: 48.1 us -> 0 us
  waiting for transfers between devices: 26.7 us -> 0 us
  matrix products: 22.8 us -> 0.36 us
  local copies, waits for them, and re-layouts: 17.5 us -> 2.8 us
    pallas_call x0 -> x2, Pallas kernels: none -> 86.9 us  [the longest x1 77.7 us: fused(): pl.pallas_call(functools.partial(fused_kernel, lax.axis_size('brick')), o...]
    mul x11 -> x1, other arithmetic: 48.5 us -> 0.01 us  [body(): coeffs = coeffs * math.sqrt(voxel_total)]
    ppermute x12 -> x0, starting transfers between devices: 48.1 us -> none  [the longest x5 36.4 us: shift_up(): return lax.ppermute(value, axis, [(i, i + 1) for i in range(size - 1)])]
    pallas_call x1, Pallas kernels: 16.3 us -> 59.8 us  [all_sum(): pl.pallas_call(functools.partial(sum_kernel, bricks, vecs), out_shape=jax...]
    ppermute x12 -> x0, waiting for transfers between devices: 26.7 us -> none  [the longest x2 26.6 us: body(): y_sent.append(lax.ppermute(y, 'vec', [(0, 1)]))]
    dot_general x4 -> x0, matrix products: 22.5 us -> none  [the longest x3 16.4 us: inner(): return jnp.einsum('in,jn->ij', left, right, precision=highest)]
    unnamed x41 -> x1, local copies, waits for them, and re-layouts: 8.33 us -> 0.07 us
    slice x10 -> x5, local copies, waits for them, and re-layouts: 8.3 us -> 0.87 us  [the longest x4 0.86 us: body(): turned = jnp.stack([pairs[0], pairs[1, :, :, ::-1]])]
  transfers between devices with their start and end apart: 12 -> 0, of which waited for: 2 -> 0; matrix products, arithmetic and copies ran while one was open for 39% -> 0% of each run, Pallas kernels for 0% -> 0%
where the time goes in v2:
time: 158 us
  Pallas kernels  147 us (93%)
  other arithmetic  6.98 us (4%)
  local copies, waits for them, and re-layouts  2.8 us (2%)
    pallas_call x1, Pallas kernels, fused(): pl.pallas_call(functools.partial(fused_kernel, lax.axis_size('brick')), o...  77.7 us
    pallas_call x1, Pallas kernels, all_sum(): pl.pallas_call(functools.partial(sum_kernel, bricks, vecs), out_shape=jax...  59.8 us
    pallas_call x1, Pallas kernels, combine(): pl.pallas_call(combine_kernel, grid=(rows // slab,), out_shape=jax.ShapeD...  9.24 us
    another operation x3, other arithmetic, body(): factor = jnp.linalg.cholesky(gram)  3.6 us

profile of v2, /device:TPU:0, one launch (start us, length us, event | category | flops | bytes accessed | tf_op | source)
XLA Modules:
  0.0 157.5 jit_solution(11080560461403099207)
XLA Ops:
  0.6 77.7 %filter_block.1 = (f32[8,32,16,128]{3,2,1,0:T(8,128)}, f32[8,32,16,128]{3,2,1,0:T(8,128)}, f32[8,32,16,128]{3,2,1,0:T(8,128)}, f32[8,32,16,128]{3,2,1,0:T(8,128)}, f32[8,128]{1,0:T(8,128)}) custom-call(s32[12,32,16,128]{3,2,1,0:T(8,128)} %lev_ref.1, s32[8,32,16,128]{3,2,1,0:T(8,128)} %start_ref.1), custom_call_target="tpu_custom_call" | custom-call | tf_op jit(solution)/shard_map/filter_block/pallas_call | solution.py:379
  78.3 59.8 %sum_blocks.1 = f32[2,8,128]{2,1,0:T(8,128)} custom-call(f32[8,128]{1,0:T(8,128)} %get-tuple-element.8.own_ref), custom_call_target="tpu_custom_call" | custom-call | tf_op jit(solution)/shard_map/sum_blocks/pallas_call | solution.py:68
  138.1 0.7 fusion.8
  138.8 0.1 slice.47
  138.9 0.1 slice.49
  139.0 0.1 rev.6
  139.1 0.1 reshape.27
  139.2 0.1 copy.8
  139.3 0.1 bitcast_add_fusion.1
  139.3 0.1 copy.11
  139.4 0.1 copy.9
  139.5 0.1 maximum_maximum_fusion
  139.6 0.1 copy.10
  139.6 0.1 fusion.2
  139.7 2.9 %cholesky.17 = f32[32,32]{1,0:T(8,128)S(1)} custom-call(f32[32,32]{1,0:T(8,128)S(1)} %fusion.2), custom_call_target="Cholesky" | custom-call | tf_op jit(solution)/shard_map/jit(cholesky)/cholesky | solution.py:423
  142.7 0.6 compare_reduce_fusion
  143.3 0.7 select_bitcast_fusion
  144.0 2.4 %custom-call.6 = f32[1,32,32]{1,2,0:T(8,128)S(1)} custom-call(f32[1,32,32]{2,1,0:T(8,128)S(1)} %get-tuple-element.13), custom_call_target="InvertDiagBlocksLowerTriangular" | custom-call | tf_op jit(solution)/shard_map/triangular_solve | solution.py:424
  146.4 0.2 fusion
  146.6 0.1 fusion.3
  146.8 0.7 slice_bitcast_fusion
  147.5 0.1 reshape.28
  147.6 0.7 reshape.29.coeff_ref
  148.3 9.2 %combine.1 = f32[8,32,16,128]{3,2,1,0:T(8,128)} custom-call(f32[8,32]{1,0:T(8,128)} %reshape.29.coeff_ref, f32[8,32,16,128]{3,2,1,0:T(8,128)} %get-tuple-element.9.x_ref, f32[8,32,16,128]{3,2,1,0:T(8,128)} %get-tuple-element.10.xo_ref, f32[8,32,16,128]{3,2,1,0:T(8,128)} %get-tuple-element.11.y_ref, f32[8,32,16,128]{3,2,1,0:T(8,128)} %get-tuple-element.12.yo_ref), custom_call_target="tpu_custom_call" | custom-call | tf_op jit(solution)/shard_map/combine/pallas_call | solution.py:458
  (9 shorter events, 0.1 us)

commit v3 on v2

--- a/solution.py
+++ b/solution.py
@@ -14,7 +14,7 @@
 MESH = pl.DeviceIdType.MESH
 
 
-def sum_kernel(bricks, vecs, own_ref, out_ref, slots, send_sem, recv_sem):
+def sum_kernel(bricks, vecs, scale, own_ref, alpha_ref, beta_ref, out_ref, slots, send_sem, recv_sem):
     brick = lax.axis_index("brick")
     vec = lax.axis_index("vec")
     total = bricks * vecs
@@ -55,21 +55,68 @@
         return carry
 
     lax.fori_loop(1, total, settle, 0)
+    halves = []
     for half in range(vecs):
         value = slots[half]
         for other in range(1, bricks):
             value = value + slots[other * vecs + half]
-        out_ref[half] = value
-
-
-def all_sum(tile):
+        halves.append(value)
+    sums = jnp.concatenate(halves, axis=0)
+    block = sums.shape[0]
+    turned = jnp.concatenate(
+        [sums, jnp.zeros((128 - block, 128), jnp.float32)], axis=0
+    ).T
+    low = lax.broadcasted_iota(jnp.int32, (block, block), 0)
+    low = low >= lax.broadcasted_iota(jnp.int32, (block, block), 1)
+    corner = jnp.where(
+        low, sums[:, 2 * block : 3 * block], turned[2 * block : 3 * block, :block]
+    )
+    gram = jnp.concatenate(
+        [
+            jnp.concatenate([sums[:, :block], turned[block : 2 * block, :block]], axis=1),
+            jnp.concatenate([sums[:, block : 2 * block], corner], axis=1),
+        ],
+        axis=0,
+    )
+    size = 2 * block
+    row = lax.broadcasted_iota(jnp.int32, (size, size), 0)
+    eye = (row == lax.broadcasted_iota(jnp.int32, (size, size), 1)).astype(jnp.float32)
+    work = jnp.concatenate(
+        [gram, eye, jnp.zeros((size, 128 - 2 * size), jnp.float32)], axis=1
+    )
+    place = lax.broadcasted_iota(jnp.int32, work.shape, 0)
+    for k in range(size):
+        root = lax.rsqrt(work[k : k + 1, k : k + 1])
+        pivot = work[k : k + 1] * root
+        factor = work[:, k : k + 1] * root
+        work = jnp.where(
+            place > k, work - factor * pivot, jnp.where(place == k, pivot, work)
+        )
+    mixed = lax.dot_general(
+        work[:block, size : size + block],
+        work[:, block:size],
+        (((1,), (1,)), ((), ())),
+        precision=highest,
+        preferred_element_type=jnp.float32,
+    )
+    alpha_ref[0] = mixed[:, :block]
+    beta_ref[0] = jnp.where(low, mixed[:, block:], 0.0)
+    out_ref[...] = work[block:, size : 2 * size] * scale
+
+
+def all_sum(tile, scale):
     bricks, vecs = lax.axis_size("brick"), lax.axis_size("vec")
     total = bricks * vecs
+    block = tile.shape[0] * vecs
     return pl.pallas_call(
-        functools.partial(sum_kernel, bricks, vecs),
-        out_shape=jax.ShapeDtypeStruct((vecs,) + tile.shape, jnp.float32),
+        functools.partial(sum_kernel, bricks, vecs, scale),
+        out_shape=(
+            jax.ShapeDtypeStruct((1, block, block), jnp.float32),
+            jax.ShapeDtypeStruct((1, block, block), jnp.float32),
+            jax.ShapeDtypeStruct((block, 2 * block), jnp.float32),
+        ),
         in_specs=[pl.BlockSpec(memory_space=pltpu.VMEM)],
-        out_specs=pl.BlockSpec(memory_space=pltpu.VMEM),
+        out_specs=(pl.BlockSpec(memory_space=pltpu.VMEM),) * 3,
         scratch_shapes=[
             pltpu.VMEM((total,) + tile.shape, jnp.float32),
             pltpu.SemaphoreType.DMA((total,)),
@@ -81,6 +128,9 @@
 
 
 ROW_STEP = 4
+X_AHEAD = 3
+OVER_AHEAD = 5
+LAG = 2
 
 
 def fused_kernel(
@@ -177,13 +227,14 @@
         for k in range(4):
             tail_up(k).start()
 
-    def push_x(c, carry):
+    def push_x(c):
         pl.when(has_high)(lambda: x_up(c).start())
         pl.when(has_low)(lambda: x_down(c).start())
+
+    for c in range(min(OVER_AHEAD, cols)):
+        if c < X_AHEAD:
+            push_x(c)
         x_over(c).start()
-        return carry
-
-    lax.fori_loop(0, cols, push_x, 0)
 
     edge = jnp.zeros((far, ny, nz), jnp.float32)
 
@@ -266,7 +317,9 @@
     pl.when(has_low)(lambda: root_up().wait_recv())
     pl.when(has_high)(lambda: root_down().wait_recv())
 
-    def first_half(c, carry):
+    def first_half(c):
+        pl.when(c + X_AHEAD < cols)(lambda: push_x(c + X_AHEAD))
+        pl.when(c + OVER_AHEAD < cols)(lambda: x_over(c + OVER_AHEAD).start())
         u_one[pl.ds(far, rows)] = root[pl.ds(far, rows)] * x_ref[c]
         pl.when(has_low)(lambda: x_up(c).wait_recv())
         u_one[pl.ds(0, far)] = root[pl.ds(0, far)] * x_low[c]
@@ -284,31 +337,31 @@
         lax.fori_loop(0, rows // step, one, 0)
         pl.when(has_high)(lambda: u_up(c).start())
         pl.when(has_low)(lambda: u_down(c).start())
-        return carry
-
-    lax.fori_loop(0, cols, first_half, 0)
 
     column = lax.broadcasted_iota(jnp.int32, tile_ref.shape, 1)
+
+    own_base = vec * cols
+    other_base = (1 - vec) * cols
+
+    def product(left_ref, right_ref, base, tile, j):
+        def add(r, total):
+            return total + left_ref[:, r] * right_ref[j, r][None]
+
+        total = lax.fori_loop(
+            0, rows, add, jnp.zeros((cols, ny, nz), jnp.float32), unroll=2
+        )
+        value = jnp.sum(jnp.sum(total, axis=1), axis=1, keepdims=True)
+        return jnp.where(column == base + j, value, tile)
 
     def products(left_ref, right_ref, base, tile, ready=None):
         def one(j, tile):
             if ready is not None:
                 ready(j)
-
-            def add(r, total):
-                return total + left_ref[:, r] * right_ref[j, r][None]
-
-            total = lax.fori_loop(
-                0, rows, add, jnp.zeros((cols, ny, nz), jnp.float32), unroll=2
-            )
-            value = jnp.sum(jnp.sum(total, axis=1), axis=1, keepdims=True)
-            return jnp.where(column == base + j, value, tile)
+            return product(left_ref, right_ref, base, tile, j)
 
         return lax.fori_loop(0, cols, one, tile)
 
-    tile = products(x_ref, x_ref, 0, jnp.zeros(tile_ref.shape, jnp.float32))
-
-    def second_half(c, carry):
+    def second_half(c):
         pl.when(has_low)(lambda: u_up(c).wait_recv())
         pl.when(has_high)(lambda: u_down(c).wait_recv())
 
@@ -319,19 +372,32 @@
 
         lax.fori_loop(0, rows // step, one, 0)
         pl.when(vec == 0)(lambda: y_over(c).start())
-        return carry
-
-    lax.fori_loop(0, cols, second_half, 0)
-    tile = products(x_ref, xo_ref, cols, tile, lambda j: x_over(j).wait_recv())
-    tile = products(y_ref, x_ref, 2 * cols, tile)
-    tile = products(y_ref, xo_ref, 3 * cols, tile)
-    tile = products(y_ref, y_ref, 4 * cols, tile)
+
+    tile_ref[...] = jnp.zeros(tile_ref.shape, jnp.float32)
+
+    def turn(c, carry):
+        pl.when(c < cols)(lambda: first_half(c))
+        pl.when(c >= LAG)(lambda: second_half(c - LAG))
+
+        @pl.when(c < cols)
+        def _():
+            tile_ref[...] = product(x_ref, x_ref, own_base, tile_ref[...], c)
+
+        return carry
+
+    lax.fori_loop(0, cols + LAG, turn, 0)
+    block = 2 * cols
+    tile = tile_ref[...]
+    tile = products(x_ref, xo_ref, other_base, tile, lambda j: x_over(j).wait_recv())
+    tile = products(y_ref, x_ref, block + own_base, tile)
+    tile = products(y_ref, xo_ref, block + other_base, tile)
+    tile = products(y_ref, y_ref, 2 * block + own_base, tile)
     tile_ref[...] = tile
 
     @pl.when(vec == 1)
     def _():
         tile_ref[...] = products(
-            y_ref, yo_ref, 5 * cols, tile_ref[...], lambda j: y_over(j).wait_recv()
+            y_ref, yo_ref, 2 * block + other_base, tile_ref[...], lambda j: y_over(j).wait_recv()
         )
 
     @pl.when(vec == 0)
@@ -401,39 +467,19 @@
 
 
 def body(levels, start_block):
-    own_cols, rows = start_block.shape[:2]
+    rows = start_block.shape[1]
     grid_shape = start_block.shape
-    vecs = lax.axis_size("vec")
-    vec = lax.axis_index("vec")
     voxel_total = lax.axis_size("brick") * rows * grid_shape[2] * grid_shape[3]
-    block = own_cols * vecs
     x, x_other, y, y_other, tile = fused(levels, start_block)
-    first = vec == 0
-    sums = all_sum(tile)
-    pairs = sums[:, :, : 6 * own_cols].reshape(vecs, own_cols, 3, 2, own_cols)
-    turned = jnp.stack([pairs[0], pairs[1, :, :, ::-1]])
-    sums = turned.reshape(block, 3, block)
-    g00 = sums[:, 0]
-    g10 = sums[:, 1]
-    g11 = jnp.tril(sums[:, 2])
-    g11 = g11 + jnp.tril(g11, -1).T
-    gram = jnp.concatenate(
-        [jnp.concatenate([g00, g10.T], axis=1), jnp.concatenate([g10, g11], axis=1)], axis=0
-    )
-    factor = jnp.linalg.cholesky(gram)
-    inverse = lax.linalg.triangular_solve(
-        factor, jnp.eye(2 * block, dtype=jnp.float32), left_side=True, lower=True
-    )
-    mixed = jnp.dot(inverse[:block, :block], factor[block:], precision=highest)
-    alpha, beta = mixed[:, :block], mixed[:, block:]
-    coeffs = lax.dynamic_slice_in_dim(inverse, block + vec * own_cols, own_cols, 0)
-    coeffs = coeffs * math.sqrt(voxel_total)
-    basis = combine(coeffs, vec, x, x_other, y, y_other)
-    return alpha[None], beta[None], basis
+    alpha, beta, coeffs = all_sum(tile, math.sqrt(voxel_total))
+    return alpha, beta, combine(coeffs, x, x_other, y, y_other)
 
 
 def combine_kernel(coeff_ref, x_ref, xo_ref, y_ref, yo_ref, out_ref):
     cols, rows = out_ref.shape[:2]
+    first = lax.axis_index("vec") * cols
+    second = cols - first
+    begins = (first, second, 2 * cols + first, 2 * cols + second)
 
     def one(r, carry):
         total = [jnp.zeros(out_ref.shape[2:], jnp.float32) for _ in range(cols)]
@@ -441,7 +487,7 @@
             for j in range(cols):
                 value = ref[j, r]
                 for i in range(cols):
-                    total[i] = total[i] + coeff_ref[i, part * cols + j] * value
+                    total[i] = total[i] + coeff_ref[first + i, begins[part] + j] * value
         for i in range(cols):
             out_ref[i, r] = total[i]
         return carry
@@ -449,10 +495,8 @@
     lax.fori_loop(0, rows, one, 0)
 
 
-def combine(coeffs, vec, x, x_other, y, y_other):
+def combine(coeffs, x, x_other, y, y_other):
     cols, rows, ny, nz = x.shape
-    parts = coeffs.reshape(cols, 2, 2, cols)
-    parts = jnp.where(vec == 0, parts, parts[:, :, ::-1]).reshape(cols, 4 * cols)
     slab = math.gcd(rows, 8)
     spec = pl.BlockSpec((cols, slab, ny, nz), lambda i: (0, i, 0, 0))
     return pl.pallas_call(
@@ -462,7 +506,7 @@
         in_specs=[pl.BlockSpec(memory_space=pltpu.SMEM)] + [spec] * 4,
         out_specs=spec,
         name="combine",
-    )(parts, x, x_other, y, y_other)
+    )(coeffs, x, x_other, y, y_other)
 
 
 def solution(mesh):

time: 158 us -> 144 us (0.911)
  other arithmetic: 6.98 us -> 0 us
  Pallas kernels: 147 us -> 142 us
  local copies, waits for them, and re-layouts: 2.8 us -> 1.21 us
    pallas_call x1, Pallas kernels: 59.8 us -> 28.1 us  [all_sum(): pl.pallas_call(functools.partial(sum_kernel, bricks, vecs, scale), out_sh...]
    pallas_call x1, Pallas kernels: 77.7 us -> 97.3 us  [fused(): pl.pallas_call(functools.partial(fused_kernel, lax.axis_size('brick')), o...]
    pallas_call x1, Pallas kernels: 9.24 us -> 16.6 us  [combine(): pl.pallas_call(combine_kernel, grid=(rows // slab,), out_shape=jax.ShapeD...]
    another operation x6 -> x0, other arithmetic: 6.72 us -> none  [the longest x3 3.6 us: body(): factor = jnp.linalg.cholesky(gram)]
where the time goes in v3:
time: 144 us
  Pallas kernels  142 us (99%)
    pallas_call x1, Pallas kernels, fused(): pl.pallas_call(functools.partial(fused_kernel, lax.axis_size('brick')), o...  97.3 us
    pallas_call x1, Pallas kernels, all_sum(): pl.pallas_call(functools.partial(sum_kernel, bricks, vecs, scale), out_sh...  28.1 us
    pallas_call x1, Pallas kernels, combine(): pl.pallas_call(combine_kernel, grid=(rows // slab,), out_shape=jax.ShapeD...  16.6 us

profile of v3, /device:TPU:0, one launch (start us, length us, event | category | flops | bytes accessed | tf_op | source)
XLA Modules:
  0.0 143.8 jit_solution(495657051826837639)
XLA Ops:
  0.6 97.3 %filter_block.1 = (f32[8,32,16,128]{3,2,1,0:T(8,128)}, f32[8,32,16,128]{3,2,1,0:T(8,128)}, f32[8,32,16,128]{3,2,1,0:T(8,128)}, f32[8,32,16,128]{3,2,1,0:T(8,128)}, f32[8,128]{1,0:T(8,128)}) custom-call(s32[12,32,16,128]{3,2,1,0:T(8,128)} %lev_ref.1, s32[8,32,16,128]{3,2,1,0:T(8,128)} %start_ref.1), custom_call_target="tpu_custom_call" | custom-call | tf_op jit(solution)/shard_map/filter_block/pallas_call | solution.py:445
  97.9 28.1 %sum_blocks.1 = (f32[1,16,16]{2,1,0:T(8,128)}, f32[1,16,16]{2,1,0:T(8,128)}, f32[16,32]{1,0:T(8,128)}) custom-call(f32[8,128]{1,0:T(8,128)} %get-tuple-element.11.own_ref), custom_call_target="tpu_custom_call" | custom-call | tf_op jit(solution)/shard_map/sum_blocks/pallas_call | solution.py:111
  126.0 0.0 copy-start.1
  126.0 0.0 copy-start
  126.0 16.6 %combine.1 = f32[8,32,16,128]{3,2,1,0:T(8,128)} custom-call(f32[16,32]{1,0:T(8,128)} %get-tuple-element.14.coeff_ref, f32[8,32,16,128]{3,2,1,0:T(8,128)} %get-tuple-element.15.x_ref, f32[8,32,16,128]{3,2,1,0:T(8,128)} %get-tuple-element.16.xo_ref, f32[8,32,16,128]{3,2,1,0:T(8,128)} %get-tuple-element.17.y_ref, f32[8,32,16,128]{3,2,1,0:T(8,128)} %get-tuple-element.18.yo_ref), custom_call_target="tpu_custom_call" | custom-call | tf_op jit(solution)/shard_map/combine/pallas_call | solution.py:502
  142.6 0.0 copy-done.1
  142.6 0.6 copy.7
  143.2 0.0 copy-done
  143.2 0.6 copy.8
Async XLA Ops:
  126.0 16.6 %copy-start.1 = (f32[1,16,16]{2,1,0:T(8,128)S(1)}, f32[1,16,16]{2,1,0:T(8,128)}, u32[]{:S(2)}) copy-start(f32[1,16,16]{2,1,0:T(8,128)} %get-tuple-element.22) | copy-start | bytes 3076
  126.0 17.2 %copy-start = (f32[1,16,16]{2,1,0:T(8,128)S(1)}, f32[1,16,16]{2,1,0:T(8,128)}, u32[]{:S(2)}) copy-start(f32[1,16,16]{2,1,0:T(8,128)} %get-tuple-element.23) | copy-start | bytes 3076

commit v4 on v3

--- a/solution.py
+++ b/solution.py
@@ -101,7 +101,13 @@
     )
     alpha_ref[0] = mixed[:, :block]
     beta_ref[0] = jnp.where(low, mixed[:, block:], 0.0)
-    out_ref[...] = work[block:, size : 2 * size] * scale
+    cols = block // 2
+    first = vec == 0
+    rest = jnp.where(first, work[block : block + cols], work[block + cols :])
+    rest = rest[:, size : 2 * size] * scale
+    order = [1, 0, 3, 2]
+    swapped = [rest[:, p * cols : (p + 1) * cols] for p in order]
+    out_ref[...] = jnp.where(first, rest, jnp.concatenate(swapped, axis=1))
 
 
 def all_sum(tile, scale):
@@ -113,7 +119,7 @@
         out_shape=(
             jax.ShapeDtypeStruct((1, block, block), jnp.float32),
             jax.ShapeDtypeStruct((1, block, block), jnp.float32),
-            jax.ShapeDtypeStruct((block, 2 * block), jnp.float32),
+            jax.ShapeDtypeStruct((block // 2, 2 * block), jnp.float32),
         ),
         in_specs=[pl.BlockSpec(memory_space=pltpu.VMEM)],
         out_specs=(pl.BlockSpec(memory_space=pltpu.VMEM),) * 3,
@@ -383,12 +389,16 @@
         def _():
             tile_ref[...] = product(x_ref, x_ref, own_base, tile_ref[...], c)
 
+        @pl.when(c >= LAG)
+        def _():
+            x_over(c - LAG).wait_recv()
+            tile_ref[...] = product(x_ref, xo_ref, other_base, tile_ref[...], c - LAG)
+
         return carry
 
     lax.fori_loop(0, cols + LAG, turn, 0)
     block = 2 * cols
     tile = tile_ref[...]
-    tile = products(x_ref, xo_ref, other_base, tile, lambda j: x_over(j).wait_recv())
     tile = products(y_ref, x_ref, block + own_base, tile)
     tile = products(y_ref, xo_ref, block + other_base, tile)
     tile = products(y_ref, y_ref, 2 * block + own_base, tile)
@@ -477,22 +487,21 @@
 
 def combine_kernel(coeff_ref, x_ref, xo_ref, y_ref, yo_ref, out_ref):
     cols, rows = out_ref.shape[:2]
-    first = lax.axis_index("vec") * cols
-    second = cols - first
-    begins = (first, second, 2 * cols + first, 2 * cols + second)
+    pair = math.gcd(rows, 2)
 
     def one(r, carry):
-        total = [jnp.zeros(out_ref.shape[2:], jnp.float32) for _ in range(cols)]
+        place = pl.ds(r * pair, pair)
+        total = [jnp.zeros((pair,) + out_ref.shape[2:], jnp.float32) for _ in range(cols)]
         for part, ref in enumerate((x_ref, xo_ref, y_ref, yo_ref)):
             for j in range(cols):
-                value = ref[j, r]
+                value = ref[j, place]
                 for i in range(cols):
-                    total[i] = total[i] + coeff_ref[first + i, begins[part] + j] * value
+                    total[i] = total[i] + coeff_ref[i, part * cols + j] * value
         for i in range(cols):
-            out_ref[i, r] = total[i]
-        return carry
-
-    lax.fori_loop(0, rows, one, 0)
+            out_ref[i, place] = total[i]
+        return carry
+
+    lax.fori_loop(0, rows // pair, one, 0)
 
 
 def combine(coeffs, x, x_other, y, y_other):

time: 144 us -> 134 us (0.931)
  Pallas kernels: 142 us -> 132 us
    pallas_call x1, Pallas kernels: 16.6 us -> 8.17 us  [combine(): pl.pallas_call(combine_kernel, grid=(rows // slab,), out_shape=jax.ShapeD...]
    pallas_call x1, Pallas kernels: 28.1 us -> 26.4 us  [all_sum(): pl.pallas_call(functools.partial(sum_kernel, bricks, vecs, scale), out_sh...]
where the time goes in v4:
time: 134 us
  Pallas kernels  132 us (99%)
    pallas_call x1, Pallas kernels, fused(): pl.pallas_call(functools.partial(fused_kernel, lax.axis_size('brick')), o...  97.3 us
    pallas_call x1, Pallas kernels, all_sum(): pl.pallas_call(functools.partial(sum_kernel, bricks, vecs, scale), out_sh...  26.4 us
    pallas_call x1, Pallas kernels, combine(): pl.pallas_call(combine_kernel, grid=(rows // slab,), out_shape=jax.ShapeD...  8.17 us

profile of v4, /device:TPU:0, one launch (start us, length us, event | category | flops | bytes accessed | tf_op | source)
XLA Modules:
  0.0 133.7 jit_solution(14221616173669011327)
XLA Ops:
  0.6 97.3 %filter_block.1 = (f32[8,32,16,128]{3,2,1,0:T(8,128)}, f32[8,32,16,128]{3,2,1,0:T(8,128)}, f32[8,32,16,128]{3,2,1,0:T(8,128)}, f32[8,32,16,128]{3,2,1,0:T(8,128)}, f32[8,128]{1,0:T(8,128)}) custom-call(s32[12,32,16,128]{3,2,1,0:T(8,128)} %lev_ref.1, s32[8,32,16,128]{3,2,1,0:T(8,128)} %start_ref.1), custom_call_target="tpu_custom_call" | custom-call | tf_op jit(solution)/shard_map/filter_block/pallas_call | solution.py:455
  97.9 26.4 %sum_blocks.1 = (f32[1,16,16]{2,1,0:T(8,128)}, f32[1,16,16]{2,1,0:T(8,128)}, f32[8,32]{1,0:T(8,128)}) custom-call(f32[8,128]{1,0:T(8,128)} %get-tuple-element.11.own_ref), custom_call_target="tpu_custom_call" | custom-call | tf_op jit(solution)/shard_map/sum_blocks/pallas_call | solution.py:117
  124.3 0.0 copy-start.1
  124.3 0.0 copy-start
  124.3 8.2 %combine.1 = f32[8,32,16,128]{3,2,1,0:T(8,128)} custom-call(f32[8,32]{1,0:T(8,128)} %get-tuple-element.14.coeff_ref, f32[8,32,16,128]{3,2,1,0:T(8,128)} %get-tuple-element.15.x_ref, f32[8,32,16,128]{3,2,1,0:T(8,128)} %get-tuple-element.16.xo_ref, f32[8,32,16,128]{3,2,1,0:T(8,128)} %get-tuple-element.17.y_ref, f32[8,32,16,128]{3,2,1,0:T(8,128)} %get-tuple-element.18.yo_ref), custom_call_target="tpu_custom_call" | custom-call | tf_op jit(solution)/shard_map/combine/pallas_call | solution.py:511
  132.5 0.0 copy-done.1
  132.5 0.6 copy.7
  133.1 0.0 copy-done
  133.1 0.6 copy.8
Async XLA Ops:
  124.3 8.2 %copy-start.1 = (f32[1,16,16]{2,1,0:T(8,128)S(1)}, f32[1,16,16]{2,1,0:T(8,128)}, u32[]{:S(2)}) copy-start(f32[1,16,16]{2,1,0:T(8,128)} %get-tuple-element.22) | copy-start | bytes 3076
  124.3 8.8 %copy-start = (f32[1,16,16]{2,1,0:T(8,128)S(1)}, f32[1,16,16]{2,1,0:T(8,128)}, u32[]{:S(2)}) copy-start(f32[1,16,16]{2,1,0:T(8,128)} %get-tuple-element.23) | copy-start | bytes 3076
